TPU v7x, 1024 devices: a whole 4x8x16 slice. The times are simulated.
1024 devices in a mesh: group: 16 (over y_hi, x, core), dom: 64 (over z, y_lo).
Axes of the slice: x: 4, y: 8 (y_hi: 2, y_lo: 4; y = y_hi * 4 + y_lo), z: 16, core: 2. Of those that a mesh axis runs over, the one named last changes fastest.
Arguments:
- u_prev: float32 [3, 2048, 2048], P(None, 'dom', 'group'), may hold values from -6 to 6
- u_now: float32 [3, 2048, 2048], P(None, 'dom', 'group'), may hold values from -6 to 6
- memory: float32 [3, 3, 2048, 2048], P(None, None, 'dom', 'group'), may hold values from -4 to 4
- modulus: float32 [2048, 2048], P('dom', 'group'), may hold values from 0.5 to 1.5
- q_weight: float32 [3, 2048, 2048], P(None, 'dom', 'group'), may hold values from 0.005 to 0.05
- adjoint_source: float32 [8, 3, 2048, 2048], P(None, None, 'dom', 'group'), may hold values from -6 to 6
- couple_src: int32 [16, 64, 64, 2], P('group', 'dom'), may hold values from -1 to 31, as said below
- couple_dst: int32 [16, 64, 64, 2], P('group', 'dom'), may hold values from -1 to 31, as said below
- couple_weight: float32 [16, 64, 64, 2], P('group', 'dom'), may hold values from 0.2 to 0.6
Outputs:
- u_end: float32 [3, 2048, 2048], P(None, 'dom', 'group')
- kernel_mu: float32 [2048, 2048], P('dom', 'group')
- kernel_q: float32 [3, 2048, 2048], P(None, 'dom', 'group')
Inputs may be any that keep to these rules, and one draw needn't show every extreme that they name: `couple_src`: -1 exactly where the slot is empty; slot s is live only if all slots below s of the same pair are; partition i never couples to itself and always fills all 2 slots towards partition (i + 1) mod 64. couple_dst[c, j, i, s] is -1 exactly where couple_src[c, i, j, s] is.
All inputs are finite; a program needn't handle non-finite values.
Results may differ from a plain program's by a relative error of at most 0.0003.
Values sent between devices are 32-bit elements; how exact they have to be, the bound alone decides.
A program may use at most 32 MiB of HBM per device.

v0:
```python
import jax
import jax.numpy as jnp
from jax import lax
from jax.sharding import PartitionSpec as P

SLS = 3
STEPS = 8


RELAX = (0.6, 0.85, 0.97)
STEP_SQ = 0.25


def padded_2(cells, sides, width):
    for axis, dim in sides:
        count = lax.axis_size(axis)
        ends = count - 1
        head = lax.slice_in_dim(cells, 0, width, axis=dim)
        tail = lax.slice_in_dim(cells, cells.shape[dim] - width, cells.shape[dim], axis=dim)
        cells = jnp.concatenate(
            [
                lax.ppermute(tail, axis, [(i, (i + 1) % count) for i in range(ends)]),
                cells,
                lax.ppermute(head, axis, [((i + 1) % count, i) for i in range(ends)]),
            ],
            axis=dim,
        )
    return cells


def laplace(field):
    padded = padded_2(field, (("group", 2), ("dom", 1)), 1)
    return (
        padded[:, 2:, 1:-1]
        + padded[:, :-2, 1:-1]
        + padded[:, 1:-1, 2:]
        + padded[:, 1:-1, :-2]
        - 4.0 * field
    )


def forward_couple(radial, picker, placer, parts):
    sent = jnp.dot(picker, radial, precision=lax.Precision.HIGHEST).reshape(
        parts, -1, radial.shape[1]
    )
    arrived = lax.all_to_all(sent, "dom", split_axis=0, concat_axis=0, tiled=True)
    return jnp.dot(placer, arrived.reshape(-1, radial.shape[1]), precision=lax.Precision.HIGHEST)


def backward_couple(radial, picker, placer, parts):
    sent = jnp.dot(placer.T, radial, precision=lax.Precision.HIGHEST).reshape(
        parts, -1, radial.shape[1]
    )
    arrived = lax.all_to_all(sent, "dom", split_axis=0, concat_axis=0, tiled=True)
    return jnp.dot(picker.T, arrived.reshape(-1, radial.shape[1]), precision=lax.Precision.HIGHEST)


def shards(
    u_prev, u_now, memory, modulus, q_weight, adjoint_source, couple_src, couple_dst, couple_weight
):
    rows = u_now.shape[1]
    parts = couple_src.shape[2]
    src_flat = couple_src.reshape(-1)
    dst_flat = couple_dst.reshape(-1)
    weight_flat = couple_weight.reshape(-1)
    row_ids = jnp.arange(rows, dtype=jnp.int32)
    picker = (src_flat[:, None] == row_ids[None, :]).astype(jnp.float32)
    placer = jnp.where(
        dst_flat[None, :] == row_ids[:, None], weight_flat[None, :], jnp.float32(0.0)
    )
    laps = []
    mems = []
    old, cur, mem = (u_prev, u_now, memory)
    for step in range(STEPS):
        lap_now = laplace(cur)
        force = modulus * lap_now
        accel = force - jnp.sum(mem, axis=0)
        accel = accel.at[0].add(forward_couple(cur[0], picker, placer, parts))
        laps.append(lap_now)
        mems.append(mem)
        fresh = 2.0 * cur - old + STEP_SQ * accel
        mem = jnp.stack([RELAX[l] * mem[l] + q_weight[l] * force for l in range(SLS)])
        old, cur = (cur, fresh)
    v_old = jnp.zeros_like(u_now)
    v_cur = jnp.zeros_like(u_now)
    adj_mem = jnp.zeros_like(memory)
    kernel_mu = jnp.zeros_like(modulus)
    kernel_q = jnp.zeros_like(q_weight)
    for step in reversed(range(STEPS)):
        force = modulus * laplace(v_cur)
        accel = force - jnp.sum(adj_mem, axis=0) + adjoint_source[step]
        accel = accel.at[0].add(backward_couple(v_cur[0], picker, placer, parts))
        fresh = 2.0 * v_cur - v_old + STEP_SQ * accel
        adj_mem = jnp.stack([RELAX[l] * adj_mem[l] + q_weight[l] * force for l in range(SLS)])
        v_old, v_cur = (v_cur, fresh)
        kernel_mu = kernel_mu + jnp.sum(v_cur * laps[step], axis=0)
        kernel_q = kernel_q + jnp.sum(v_cur[None] * mems[step], axis=1)
    scale = 1.0 / (3.0 * STEPS)
    return (cur, kernel_mu * scale, kernel_q * scale)


def solution(mesh):
    in_specs = (
        P(None, "dom", "group"),
        P(None, "dom", "group"),
        P(None, None, "dom", "group"),
        P("dom", "group"),
        P(None, "dom", "group"),
        P(None, None, "dom", "group"),
        P("group", "dom", None, None),
        P("group", "dom", None, None),
        P("group", "dom", None, None),
    )
    out_specs = (P(None, "dom", "group"), P("dom", "group"), P(None, "dom", "group"))
    return jax.shard_map(shards, mesh=mesh, in_specs=in_specs, out_specs=out_specs, check_vma=False)
```

profile of v0, /device:TPU:56, one launch (start us, length us, event | category | flops | bytes accessed | tf_op | source)
XLA Modules:
  0.0 667.5 jit_solution(11701068737221799713)
XLA Ops:
  10.7 22.6 %all-to-all-start.8 = ((f32[64,2,128]{2,1,0:T(2,128)}), f32[64,2,128]{2,1,0:T(2,128)S(1)}, u32[]{:S(2)}, u32[]{:S(2)}) async-start(f32[64,2,128]{2,1,0:T(2,128)} %copy.45), calls=%async_computation.8 | async-start | bytes 131072 | tf_op jit(solution)/shard_map/all_to_all | solution.py:54
  46.7 8.4 %collective-permute-start.37 = (f32[3,32,1]{2,1,0:T(8,128)S(1)}, f32[3,32,1]{2,1,0:T(8,128)S(1)}, u32[]{:S(2)}, u32[]{:S(2)}) collective-permute-start(f32[3,32,1]{2,1,0:T(8,128)S(1)} %get-tuple-element.320), channel_id=1, source_target_pairs={{64,0},{128,64},{192,128},{256,192},{320,256},{384,320},{448,384},... | collective-permute-start | bytes 1160 | tf_op jit(solution)/shard_map/ppermute | solution.py:24
  58.0 14.0 %all-to-all-start.9 = ((f32[64,2,128]{2,1,0:T(2,128)}), f32[64,2,128]{2,1,0:T(2,128)S(1)}, u32[]{:S(2)}, u32[]{:S(2)}) async-start(f32[64,2,128]{2,1,0:T(2,128)} %copy.46), calls=%async_computation.9 | async-start | bytes 131072 | tf_op jit(solution)/shard_map/all_to_all | solution.py:54
  85.4 8.2 %collective-permute-start.41 = (f32[3,32,1]{2,1,0:T(8,128)S(1)}, f32[3,32,1]{2,1,0:T(8,128)S(1)}, u32[]{:S(2)}, u32[]{:S(2)}) collective-permute-start(f32[3,32,1]{2,1,0:T(8,128)S(1)} %get-tuple-element.318), channel_id=1, source_target_pairs={{64,0},{128,64},{192,128},{256,192},{320,256},{384,320},{448,384},... | collective-permute-start | bytes 1160 | tf_op jit(solution)/shard_map/ppermute | solution.py:24
  96.5 14.0 %all-to-all-start.10 = ((f32[64,2,128]{2,1,0:T(2,128)}), f32[64,2,128]{2,1,0:T(2,128)S(1)}, u32[]{:S(2)}, u32[]{:S(2)}) async-start(f32[64,2,128]{2,1,0:T(2,128)} %copy.47), calls=%async_computation.10 | async-start | bytes 131072 | tf_op jit(solution)/shard_map/all_to_all | solution.py:54
  123.9 8.2 %collective-permute-start.45 = (f32[3,32,1]{2,1,0:T(8,128)S(1)}, f32[3,32,1]{2,1,0:T(8,128)S(1)}, u32[]{:S(2)}, u32[]{:S(2)}) collective-permute-start(f32[3,32,1]{2,1,0:T(8,128)S(1)} %get-tuple-element.316), channel_id=1, source_target_pairs={{64,0},{128,64},{192,128},{256,192},{320,256},{384,320},{448,384},... | collective-permute-start | bytes 1160 | tf_op jit(solution)/shard_map/ppermute | solution.py:24
  135.0 14.0 %all-to-all-start.11 = ((f32[64,2,128]{2,1,0:T(2,128)}), f32[64,2,128]{2,1,0:T(2,128)S(1)}, u32[]{:S(2)}, u32[]{:S(2)}) async-start(f32[64,2,128]{2,1,0:T(2,128)} %copy.48), calls=%async_computation.11 | async-start | bytes 131072 | tf_op jit(solution)/shard_map/all_to_all | solution.py:54
  162.4 8.2 %collective-permute-start.49 = (f32[3,32,1]{2,1,0:T(8,128)S(1)}, f32[3,32,1]{2,1,0:T(8,128)S(1)}, u32[]{:S(2)}, u32[]{:S(2)}) collective-permute-start(f32[3,32,1]{2,1,0:T(8,128)S(1)} %get-tuple-element.314), channel_id=1, source_target_pairs={{64,0},{128,64},{192,128},{256,192},{320,256},{384,320},{448,384},... | collective-permute-start | bytes 1160 | tf_op jit(solution)/shard_map/ppermute | solution.py:24
  173.5 14.0 %all-to-all-start.12 = ((f32[64,2,128]{2,1,0:T(2,128)}), f32[64,2,128]{2,1,0:T(2,128)S(1)}, u32[]{:S(2)}, u32[]{:S(2)}) async-start(f32[64,2,128]{2,1,0:T(2,128)} %copy.49), calls=%async_computation.12 | async-start | bytes 131072 | tf_op jit(solution)/shard_map/all_to_all | solution.py:54
  200.9 8.2 %collective-permute-start.53 = (f32[3,32,1]{2,1,0:T(8,128)S(1)}, f32[3,32,1]{2,1,0:T(8,128)S(1)}, u32[]{:S(2)}, u32[]{:S(2)}) collective-permute-start(f32[3,32,1]{2,1,0:T(8,128)S(1)} %get-tuple-element.312), channel_id=1, source_target_pairs={{64,0},{128,64},{192,128},{256,192},{320,256},{384,320},{448,384},... | collective-permute-start | bytes 1160 | tf_op jit(solution)/shard_map/ppermute | solution.py:24
  212.0 14.0 %all-to-all-start.13 = ((f32[64,2,128]{2,1,0:T(2,128)}), f32[64,2,128]{2,1,0:T(2,128)S(1)}, u32[]{:S(2)}, u32[]{:S(2)}) async-start(f32[64,2,128]{2,1,0:T(2,128)} %copy.50), calls=%async_computation.13 | async-start | bytes 131072 | tf_op jit(solution)/shard_map/all_to_all | solution.py:54
  234.8 8.5 %collective-permute-start.1 = (f32[3,32,1]{2,1,0:T(8,128)S(1)}, f32[3,32,1]{2,1,0:T(8,128)S(1)}, u32[]{:S(2)}, u32[]{:S(2)}) collective-permute-start(f32[3,32,1]{2,1,0:T(8,128)S(1)} %get-tuple-element.306), channel_id=1, source_target_pairs={{64,0},{128,64},{192,128},{256,192},{320,256},{384,320},{448,384},... | collective-permute-start | bytes 1160 | tf_op jit(solution)/shard_map/ppermute | solution.py:24
  245.8 9.7 %collective-permute-start.57 = (f32[3,32,1]{2,1,0:T(8,128)S(1)}, f32[3,32,1]{2,1,0:T(8,128)S(1)}, u32[]{:S(2)}, u32[]{:S(2)}) collective-permute-start(f32[3,32,1]{2,1,0:T(8,128)S(1)} %get-tuple-element.310), channel_id=1, source_target_pairs={{64,0},{128,64},{192,128},{256,192},{320,256},{384,320},{448,384},... | collective-permute-start | bytes 1160 | tf_op jit(solution)/shard_map/ppermute | solution.py:24
  258.4 15.4 %all-to-all-start.14 = ((f32[64,2,128]{2,1,0:T(2,128)}), f32[64,2,128]{2,1,0:T(2,128)S(1)}, u32[]{:S(2)}, u32[]{:S(2)}) async-start(f32[64,2,128]{2,1,0:T(2,128)} %copy.51), calls=%async_computation.14 | async-start | bytes 131072 | tf_op jit(solution)/shard_map/all_to_all | solution.py:54
  287.0 8.4 %collective-permute-start.61 = (f32[3,32,1]{2,1,0:T(8,128)S(1)}, f32[3,32,1]{2,1,0:T(8,128)S(1)}, u32[]{:S(2)}, u32[]{:S(2)}) collective-permute-start(f32[3,32,1]{2,1,0:T(8,128)S(1)} %get-tuple-element.308), channel_id=1, source_target_pairs={{64,0},{128,64},{192,128},{256,192},{320,256},{384,320},{448,384},... | collective-permute-start | bytes 1160 | tf_op jit(solution)/shard_map/ppermute | solution.py:24
  298.3 13.9 %all-to-all-start.15 = ((f32[64,2,128]{2,1,0:T(2,128)}), f32[64,2,128]{2,1,0:T(2,128)S(1)}, u32[]{:S(2)}, u32[]{:S(2)}) async-start(f32[64,2,128]{2,1,0:T(2,128)} %copy.52), calls=%async_computation.15 | async-start | bytes 131072 | tf_op jit(solution)/shard_map/all_to_all | solution.py:54
  329.8 15.7 %all-to-all-start = ((f32[64,2,128]{2,1,0:T(2,128)}), f32[64,2,128]{2,1,0:T(2,128)S(1)}, u32[]{:S(2)}, u32[]{:S(2)}) async-start(f32[64,2,128]{2,1,0:T(2,128)} %copy.36), calls=%async_computation | async-start | bytes 131072 | tf_op jit(solution)/shard_map/all_to_all | solution.py:46
  346.7 11.7 %all-to-all-done = f32[64,2,128]{2,1,0:T(2,128)S(1)} async-done(((f32[64,2,128]{2,1,0:T(2,128)}), f32[64,2,128]{2,1,0:T(2,128)S(1)}, u32[]{:S(2)}, u32[]{:S(2)}) %all-to-all-start) | async-done | bytes 65568 | tf_op jit(solution)/shard_map/all_to_all | solution.py:46
  367.8 9.6 %collective-permute-done.4 = f32[3,32,1]{2,1,0:T(8,128)S(1)} collective-permute-done((f32[3,32,1]{2,1,0:T(8,128)S(1)}, f32[3,32,1]{2,1,0:T(8,128)S(1)}, u32[]{:S(2)}, u32[]{:S(2)}) %collective-permute-start.4) | collective-permute-done | bytes 416 | tf_op jit(solution)/shard_map/ppermute | solution.py:22
  394.2 12.8 %all-to-all-done.1 = f32[64,2,128]{2,1,0:T(2,128)S(1)} async-done(((f32[64,2,128]{2,1,0:T(2,128)}), f32[64,2,128]{2,1,0:T(2,128)S(1)}, u32[]{:S(2)}, u32[]{:S(2)}) %all-to-all-start.1) | async-done | bytes 65568 | tf_op jit(solution)/shard_map/all_to_all | solution.py:46
  411.6 9.1 %collective-permute-done.8 = f32[3,32,1]{2,1,0:T(8,128)S(1)} collective-permute-done((f32[3,32,1]{2,1,0:T(8,128)S(1)}, f32[3,32,1]{2,1,0:T(8,128)S(1)}, u32[]{:S(2)}, u32[]{:S(2)}) %collective-permute-start.8) | collective-permute-done | bytes 416 | tf_op jit(solution)/shard_map/ppermute | solution.py:22
  437.5 12.8 %all-to-all-done.2 = f32[64,2,128]{2,1,0:T(2,128)S(1)} async-done(((f32[64,2,128]{2,1,0:T(2,128)}), f32[64,2,128]{2,1,0:T(2,128)S(1)}, u32[]{:S(2)}, u32[]{:S(2)}) %all-to-all-start.2) | async-done | bytes 65568 | tf_op jit(solution)/shard_map/all_to_all | solution.py:46
  454.9 9.1 %collective-permute-done.12 = f32[3,32,1]{2,1,0:T(8,128)S(1)} collective-permute-done((f32[3,32,1]{2,1,0:T(8,128)S(1)}, f32[3,32,1]{2,1,0:T(8,128)S(1)}, u32[]{:S(2)}, u32[]{:S(2)}) %collective-permute-start.12) | collective-permute-done | bytes 416 | tf_op jit(solution)/shard_map/ppermute | solution.py:22
  480.7 12.8 %all-to-all-done.3 = f32[64,2,128]{2,1,0:T(2,128)S(1)} async-done(((f32[64,2,128]{2,1,0:T(2,128)}), f32[64,2,128]{2,1,0:T(2,128)S(1)}, u32[]{:S(2)}, u32[]{:S(2)}) %all-to-all-start.3) | async-done | bytes 65568 | tf_op jit(solution)/shard_map/all_to_all | solution.py:46
  498.1 9.1 %collective-permute-done.16 = f32[3,32,1]{2,1,0:T(8,128)S(1)} collective-permute-done((f32[3,32,1]{2,1,0:T(8,128)S(1)}, f32[3,32,1]{2,1,0:T(8,128)S(1)}, u32[]{:S(2)}, u32[]{:S(2)}) %collective-permute-start.16) | collective-permute-done | bytes 416 | tf_op jit(solution)/shard_map/ppermute | solution.py:22
  523.9 12.8 %all-to-all-done.4 = f32[64,2,128]{2,1,0:T(2,128)S(1)} async-done(((f32[64,2,128]{2,1,0:T(2,128)}), f32[64,2,128]{2,1,0:T(2,128)S(1)}, u32[]{:S(2)}, u32[]{:S(2)}) %all-to-all-start.4) | async-done | bytes 65568 | tf_op jit(solution)/shard_map/all_to_all | solution.py:46
  541.4 9.1 %collective-permute-done.20 = f32[3,32,1]{2,1,0:T(8,128)S(1)} collective-permute-done((f32[3,32,1]{2,1,0:T(8,128)S(1)}, f32[3,32,1]{2,1,0:T(8,128)S(1)}, u32[]{:S(2)}, u32[]{:S(2)}) %collective-permute-start.20) | collective-permute-done | bytes 416 | tf_op jit(solution)/shard_map/ppermute | solution.py:22
  567.4 12.8 %all-to-all-done.5 = f32[64,2,128]{2,1,0:T(2,128)S(1)} async-done(((f32[64,2,128]{2,1,0:T(2,128)}), f32[64,2,128]{2,1,0:T(2,128)S(1)}, u32[]{:S(2)}, u32[]{:S(2)}) %all-to-all-start.5) | async-done | bytes 65568 | tf_op jit(solution)/shard_map/all_to_all | solution.py:46
  584.8 9.1 %collective-permute-done.24 = f32[3,32,1]{2,1,0:T(8,128)S(1)} collective-permute-done((f32[3,32,1]{2,1,0:T(8,128)S(1)}, f32[3,32,1]{2,1,0:T(8,128)S(1)}, u32[]{:S(2)}, u32[]{:S(2)}) %collective-permute-start.24) | collective-permute-done | bytes 416 | tf_op jit(solution)/shard_map/ppermute | solution.py:22
  610.7 12.7 %all-to-all-done.6 = f32[64,2,128]{2,1,0:T(2,128)S(1)} async-done(((f32[64,2,128]{2,1,0:T(2,128)}), f32[64,2,128]{2,1,0:T(2,128)S(1)}, u32[]{:S(2)}, u32[]{:S(2)}) %all-to-all-start.6) | async-done | bytes 65568 | tf_op jit(solution)/shard_map/all_to_all | solution.py:46
  628.7 8.5 %collective-permute-done.28 = f32[3,32,1]{2,1,0:T(8,128)S(1)} collective-permute-done((f32[3,32,1]{2,1,0:T(8,128)S(1)}, f32[3,32,1]{2,1,0:T(8,128)S(1)}, u32[]{:S(2)}, u32[]{:S(2)}) %collective-permute-start.28) | collective-permute-done | bytes 416 | tf_op jit(solution)/shard_map/ppermute | solution.py:22
  654.5 12.1 %all-to-all-done.7 = f32[64,2,128]{2,1,0:T(2,128)S(1)} async-done(((f32[64,2,128]{2,1,0:T(2,128)}), f32[64,2,128]{2,1,0:T(2,128)S(1)}, u32[]{:S(2)}, u32[]{:S(2)}) %all-to-all-start.7) | async-done | bytes 65568 | tf_op jit(solution)/shard_map/all_to_all | solution.py:46
  (283 shorter events, 295.9 us)
Async XLA Ops:
  0.7 32.7 %collective-permute-start.33 = (f32[3,32,1]{2,1,0:T(8,128)S(1)}, f32[3,32,1]{2,1,0:T(8,128)S(1)}, u32[]{:S(2)}, u32[]{:S(2)}) collective-permute-start(f32[3,32,1]{2,1,0:T(8,128)S(1)} %broadcast.415), channel_id=1, source_target_pairs={{64,0},{128,64},{192,128},{256,192},{320,256},{384,320},{448,384},... | collective-permute-start | bytes 1160 | tf_op jit(solution)/shard_map/ppermute | solution.py:24
  7.1 26.2 %collective-permute-start.32 = (f32[3,32,1]{2,1,0:T(8,128)S(1)}, f32[3,32,1]{2,1,0:T(8,128)S(1)}, u32[]{:S(2)}, u32[]{:S(2)}) collective-permute-start(f32[3,32,1]{2,1,0:T(8,128)S(1)} %broadcast.415), channel_id=1, source_target_pairs={{0,64},{64,128},{128,192},{192,256},{256,320},{320,384},{384,448},... | collective-permute-start | bytes 1160 | tf_op jit(solution)/shard_map/ppermute | solution.py:22
  10.7 35.6 %all-to-all-start.8 = ((f32[64,2,128]{2,1,0:T(2,128)}), f32[64,2,128]{2,1,0:T(2,128)S(1)}, u32[]{:S(2)}, u32[]{:S(2)}) async-start(f32[64,2,128]{2,1,0:T(2,128)} %copy.45), calls=%async_computation.8 | async-start | bytes 131072 | tf_op jit(solution)/shard_map/all_to_all | solution.py:54
  46.7 25.3 %collective-permute-start.37 = (f32[3,32,1]{2,1,0:T(8,128)S(1)}, f32[3,32,1]{2,1,0:T(8,128)S(1)}, u32[]{:S(2)}, u32[]{:S(2)}) collective-permute-start(f32[3,32,1]{2,1,0:T(8,128)S(1)} %get-tuple-element.320), channel_id=1, source_target_pairs={{64,0},{128,64},{192,128},{256,192},{320,256},{384,320},{448,384},... | collective-permute-start | bytes 1160 | tf_op jit(solution)/shard_map/ppermute | solution.py:24
  58.0 27.0 %all-to-all-start.9 = ((f32[64,2,128]{2,1,0:T(2,128)}), f32[64,2,128]{2,1,0:T(2,128)S(1)}, u32[]{:S(2)}, u32[]{:S(2)}) async-start(f32[64,2,128]{2,1,0:T(2,128)} %copy.46), calls=%async_computation.9 | async-start | bytes 131072 | tf_op jit(solution)/shard_map/all_to_all | solution.py:54
  85.4 25.1 %collective-permute-start.41 = (f32[3,32,1]{2,1,0:T(8,128)S(1)}, f32[3,32,1]{2,1,0:T(8,128)S(1)}, u32[]{:S(2)}, u32[]{:S(2)}) collective-permute-start(f32[3,32,1]{2,1,0:T(8,128)S(1)} %get-tuple-element.318), channel_id=1, source_target_pairs={{64,0},{128,64},{192,128},{256,192},{320,256},{384,320},{448,384},... | collective-permute-start | bytes 1160 | tf_op jit(solution)/shard_map/ppermute | solution.py:24
  96.5 27.0 %all-to-all-start.10 = ((f32[64,2,128]{2,1,0:T(2,128)}), f32[64,2,128]{2,1,0:T(2,128)S(1)}, u32[]{:S(2)}, u32[]{:S(2)}) async-start(f32[64,2,128]{2,1,0:T(2,128)} %copy.47), calls=%async_computation.10 | async-start | bytes 131072 | tf_op jit(solution)/shard_map/all_to_all | solution.py:54
  123.9 25.1 %collective-permute-start.45 = (f32[3,32,1]{2,1,0:T(8,128)S(1)}, f32[3,32,1]{2,1,0:T(8,128)S(1)}, u32[]{:S(2)}, u32[]{:S(2)}) collective-permute-start(f32[3,32,1]{2,1,0:T(8,128)S(1)} %get-tuple-element.316), channel_id=1, source_target_pairs={{64,0},{128,64},{192,128},{256,192},{320,256},{384,320},{448,384},... | collective-permute-start | bytes 1160 | tf_op jit(solution)/shard_map/ppermute | solution.py:24
  135.0 27.0 %all-to-all-start.11 = ((f32[64,2,128]{2,1,0:T(2,128)}), f32[64,2,128]{2,1,0:T(2,128)S(1)}, u32[]{:S(2)}, u32[]{:S(2)}) async-start(f32[64,2,128]{2,1,0:T(2,128)} %copy.48), calls=%async_computation.11 | async-start | bytes 131072 | tf_op jit(solution)/shard_map/all_to_all | solution.py:54
  162.4 25.1 %collective-permute-start.49 = (f32[3,32,1]{2,1,0:T(8,128)S(1)}, f32[3,32,1]{2,1,0:T(8,128)S(1)}, u32[]{:S(2)}, u32[]{:S(2)}) collective-permute-start(f32[3,32,1]{2,1,0:T(8,128)S(1)} %get-tuple-element.314), channel_id=1, source_target_pairs={{64,0},{128,64},{192,128},{256,192},{320,256},{384,320},{448,384},... | collective-permute-start | bytes 1160 | tf_op jit(solution)/shard_map/ppermute | solution.py:24
  173.5 27.0 %all-to-all-start.12 = ((f32[64,2,128]{2,1,0:T(2,128)}), f32[64,2,128]{2,1,0:T(2,128)S(1)}, u32[]{:S(2)}, u32[]{:S(2)}) async-start(f32[64,2,128]{2,1,0:T(2,128)} %copy.49), calls=%async_computation.12 | async-start | bytes 131072 | tf_op jit(solution)/shard_map/all_to_all | solution.py:54
  200.9 25.1 %collective-permute-start.53 = (f32[3,32,1]{2,1,0:T(8,128)S(1)}, f32[3,32,1]{2,1,0:T(8,128)S(1)}, u32[]{:S(2)}, u32[]{:S(2)}) collective-permute-start(f32[3,32,1]{2,1,0:T(8,128)S(1)} %get-tuple-element.312), channel_id=1, source_target_pairs={{64,0},{128,64},{192,128},{256,192},{320,256},{384,320},{448,384},... | collective-permute-start | bytes 1160 | tf_op jit(solution)/shard_map/ppermute | solution.py:24
  212.0 33.4 %all-to-all-start.13 = ((f32[64,2,128]{2,1,0:T(2,128)}), f32[64,2,128]{2,1,0:T(2,128)S(1)}, u32[]{:S(2)}, u32[]{:S(2)}) async-start(f32[64,2,128]{2,1,0:T(2,128)} %copy.50), calls=%async_computation.13 | async-start | bytes 131072 | tf_op jit(solution)/shard_map/all_to_all | solution.py:54
  226.1 19.1 %collective-permute-start.54 = (f32[3,1,130]{2,1,0:T(1,128)S(1)}, f32[3,1,130]{2,1,0:T(1,128)S(1)}, u32[]{:S(2)}, u32[]{:S(2)}) collective-permute-start(f32[3,1,130]{2,1,0:T(1,128)S(1)} %get-tuple-element.276), channel_id=1, source_target_pairs={{1,0},{2,1},{3,2},{4,3},{5,4},{6,5},{7,6},{8,7},{9,8},{10,9},{11,1... | collective-permute-start | bytes 4688 | tf_op jit(solution)/shard_map/ppermute | solution.py:24
  234.8 86.2 %collective-permute-start.1 = (f32[3,32,1]{2,1,0:T(8,128)S(1)}, f32[3,32,1]{2,1,0:T(8,128)S(1)}, u32[]{:S(2)}, u32[]{:S(2)}) collective-permute-start(f32[3,32,1]{2,1,0:T(8,128)S(1)} %get-tuple-element.306), channel_id=1, source_target_pairs={{64,0},{128,64},{192,128},{256,192},{320,256},{384,320},{448,384},... | collective-permute-start | bytes 1160 | tf_op jit(solution)/shard_map/ppermute | solution.py:24
  243.3 77.6 %collective-permute-start = (f32[3,32,1]{2,1,0:T(8,128)S(1)}, f32[3,32,1]{2,1,0:T(8,128)S(1)}, u32[]{:S(2)}, u32[]{:S(2)}) collective-permute-start(f32[3,32,1]{2,1,0:T(8,128)S(1)} %get-tuple-element.307), channel_id=1, source_target_pairs={{0,64},{64,128},{128,192},{192,256},{256,320},{320,384},{384,448},... | collective-permute-start | bytes 1160 | tf_op jit(solution)/shard_map/ppermute | solution.py:22
  245.8 28.0 %collective-permute-start.57 = (f32[3,32,1]{2,1,0:T(8,128)S(1)}, f32[3,32,1]{2,1,0:T(8,128)S(1)}, u32[]{:S(2)}, u32[]{:S(2)}) collective-permute-start(f32[3,32,1]{2,1,0:T(8,128)S(1)} %get-tuple-element.310), channel_id=1, source_target_pairs={{64,0},{128,64},{192,128},{256,192},{320,256},{384,320},{448,384},... | collective-permute-start | bytes 1160 | tf_op jit(solution)/shard_map/ppermute | solution.py:24
  255.5 18.3 %collective-permute-start.56 = (f32[3,32,1]{2,1,0:T(8,128)S(1)}, f32[3,32,1]{2,1,0:T(8,128)S(1)}, u32[]{:S(2)}, u32[]{:S(2)}) collective-permute-start(f32[3,32,1]{2,1,0:T(8,128)S(1)} %get-tuple-element.311), channel_id=1, source_target_pairs={{0,64},{64,128},{128,192},{192,256},{256,320},{320,384},{384,448},... | collective-permute-start | bytes 1160 | tf_op jit(solution)/shard_map/ppermute | solution.py:22
  258.4 28.3 %all-to-all-start.14 = ((f32[64,2,128]{2,1,0:T(2,128)}), f32[64,2,128]{2,1,0:T(2,128)S(1)}, u32[]{:S(2)}, u32[]{:S(2)}) async-start(f32[64,2,128]{2,1,0:T(2,128)} %copy.51), calls=%async_computation.14 | async-start | bytes 131072 | tf_op jit(solution)/shard_map/all_to_all | solution.py:54
  287.0 25.2 %collective-permute-start.61 = (f32[3,32,1]{2,1,0:T(8,128)S(1)}, f32[3,32,1]{2,1,0:T(8,128)S(1)}, u32[]{:S(2)}, u32[]{:S(2)}) collective-permute-start(f32[3,32,1]{2,1,0:T(8,128)S(1)} %get-tuple-element.308), channel_id=1, source_target_pairs={{64,0},{128,64},{192,128},{256,192},{320,256},{384,320},{448,384},... | collective-permute-start | bytes 1160 | tf_op jit(solution)/shard_map/ppermute | solution.py:24
  298.3 31.5 %all-to-all-start.15 = ((f32[64,2,128]{2,1,0:T(2,128)}), f32[64,2,128]{2,1,0:T(2,128)S(1)}, u32[]{:S(2)}, u32[]{:S(2)}) async-start(f32[64,2,128]{2,1,0:T(2,128)} %copy.52), calls=%async_computation.15 | async-start | bytes 131072 | tf_op jit(solution)/shard_map/all_to_all | solution.py:54
  312.4 17.2 %collective-permute-start.62 = (f32[3,1,130]{2,1,0:T(1,128)S(1)}, f32[3,1,130]{2,1,0:T(1,128)S(1)}, u32[]{:S(2)}, u32[]{:S(2)}) collective-permute-start(f32[3,1,130]{2,1,0:T(1,128)S(1)} %get-tuple-element.272), channel_id=1, source_target_pairs={{1,0},{2,1},{3,2},{4,3},{5,4},{6,5},{7,6},{8,7},{9,8},{10,9},{11,1... | collective-permute-start | bytes 4688 | tf_op jit(solution)/shard_map/ppermute | solution.py:24
  321.0 24.7 %collective-permute-start.2 = (f32[3,1,130]{2,1,0:T(1,128)S(1)}, f32[3,1,130]{2,1,0:T(1,128)S(1)}, u32[]{:S(2)}, u32[]{:S(2)}) collective-permute-start(f32[3,1,130]{2,1,0:T(1,128)S(1)} %get-tuple-element.270), channel_id=1, source_target_pairs={{1,0},{2,1},{3,2},{4,3},{5,4},{6,5},{7,6},{8,7},{9,8},{10,9},{11,1... | collective-permute-start | bytes 4688 | tf_op jit(solution)/shard_map/ppermute | solution.py:24
  323.0 22.8 %collective-permute-start.3 = (f32[3,1,130]{2,1,0:T(1,128)S(1)}, f32[3,1,130]{2,1,0:T(1,128)S(1)}, u32[]{:S(2)}, u32[]{:S(2)}) collective-permute-start(f32[3,1,130]{2,1,0:T(1,128)S(1)} %get-tuple-element.271), channel_id=1, source_target_pairs={{0,1},{1,2},{2,3},{3,4},{4,5},{5,6},{6,7},{7,8},{8,9},{9,10},{10,1... | collective-permute-start | bytes 4688 | tf_op jit(solution)/shard_map/ppermute | solution.py:22
  329.8 28.7 %all-to-all-start = ((f32[64,2,128]{2,1,0:T(2,128)}), f32[64,2,128]{2,1,0:T(2,128)S(1)}, u32[]{:S(2)}, u32[]{:S(2)}) async-start(f32[64,2,128]{2,1,0:T(2,128)} %copy.36), calls=%async_computation | async-start | bytes 131072 | tf_op jit(solution)/shard_map/all_to_all | solution.py:46
  387.0 20.0 %all-to-all-start.1 = ((f32[64,2,128]{2,1,0:T(2,128)}), f32[64,2,128]{2,1,0:T(2,128)S(1)}, u32[]{:S(2)}, u32[]{:S(2)}) async-start(f32[64,2,128]{2,1,0:T(2,128)} %copy.37), calls=%async_computation.1 | async-start | bytes 131072 | tf_op jit(solution)/shard_map/all_to_all | solution.py:46
  430.3 19.9 %all-to-all-start.2 = ((f32[64,2,128]{2,1,0:T(2,128)}), f32[64,2,128]{2,1,0:T(2,128)S(1)}, u32[]{:S(2)}, u32[]{:S(2)}) async-start(f32[64,2,128]{2,1,0:T(2,128)} %copy.38), calls=%async_computation.2 | async-start | bytes 131072 | tf_op jit(solution)/shard_map/all_to_all | solution.py:46
  473.5 19.9 %all-to-all-start.3 = ((f32[64,2,128]{2,1,0:T(2,128)}), f32[64,2,128]{2,1,0:T(2,128)S(1)}, u32[]{:S(2)}, u32[]{:S(2)}) async-start(f32[64,2,128]{2,1,0:T(2,128)} %copy.39), calls=%async_computation.3 | async-start | bytes 131072 | tf_op jit(solution)/shard_map/all_to_all | solution.py:46
  516.8 19.9 %all-to-all-start.4 = ((f32[64,2,128]{2,1,0:T(2,128)}), f32[64,2,128]{2,1,0:T(2,128)S(1)}, u32[]{:S(2)}, u32[]{:S(2)}) async-start(f32[64,2,128]{2,1,0:T(2,128)} %copy.40), calls=%async_computation.4 | async-start | bytes 131072 | tf_op jit(solution)/shard_map/all_to_all | solution.py:46
  560.0 20.2 %all-to-all-start.5 = ((f32[64,2,128]{2,1,0:T(2,128)}), f32[64,2,128]{2,1,0:T(2,128)S(1)}, u32[]{:S(2)}, u32[]{:S(2)}) async-start(f32[64,2,128]{2,1,0:T(2,128)} %copy.41), calls=%async_computation.5 | async-start | bytes 131072 | tf_op jit(solution)/shard_map/all_to_all | solution.py:46
  603.5 19.9 %all-to-all-start.6 = ((f32[64,2,128]{2,1,0:T(2,128)}), f32[64,2,128]{2,1,0:T(2,128)S(1)}, u32[]{:S(2)}, u32[]{:S(2)}) async-start(f32[64,2,128]{2,1,0:T(2,128)} %copy.42), calls=%async_computation.6 | async-start | bytes 131072 | tf_op jit(solution)/shard_map/all_to_all | solution.py:46
  646.7 19.9 %all-to-all-start.7 = ((f32[64,2,128]{2,1,0:T(2,128)}), f32[64,2,128]{2,1,0:T(2,128)S(1)}, u32[]{:S(2)}, u32[]{:S(2)}) async-start(f32[64,2,128]{2,1,0:T(2,128)} %copy.43), calls=%async_computation.7 | async-start | bytes 131072 | tf_op jit(solution)/shard_map/all_to_all | solution.py:46
  (57 other events, 648.4 us)
where the time goes:
time: 670 us; the launch traced here: 667 us
  starting transfers between devices  449 us (67%)
  waiting for transfers between devices  187 us (28%)
  local copies, waits for them, and re-layouts  14.2 us (2%)
  matrix products  8.46 us (1%)
    ppermute x32, starting transfers between devices, padded_2(): lax.ppermute(head, axis, [((i + 1) % count, i) for i in range(ends)])  135 us
    ppermute x32, starting transfers between devices, padded_2(): lax.ppermute(tail, axis, [(i, (i + 1) % count) for i in range(ends)])  128 us
    all_to_all x8, starting transfers between devices, backward_couple(): lax.all_to_all(sent, 'dom', split_axis=0, concat_axis=0, tiled=True)  122 us
    all_to_all x8, waiting for transfers between devices, forward_couple(): lax.all_to_all(sent, 'dom', split_axis=0, concat_axis=0, tiled=True)  100 us
    ppermute x32, waiting for transfers between devices, padded_2(): lax.ppermute(tail, axis, [(i, (i + 1) % count) for i in range(ends)])  69.6 us
    all_to_all x8, starting transfers between devices, forward_couple(): lax.all_to_all(sent, 'dom', split_axis=0, concat_axis=0, tiled=True)  64.6 us
    all_to_all x8, waiting for transfers between devices, backward_couple(): lax.all_to_all(sent, 'dom', split_axis=0, concat_axis=0, tiled=True)  17 us
  transfers between devices with their start and end apart: 80, of which 26 were waited for; matrix products, arithmetic and copies ran while one was open for 3% of the time, Pallas kernels for 0%

commit v1 on v0

v1 whole, which is shorter than its diff:
```python
import functools

import jax
import jax.numpy as jnp
from jax import lax
from jax.experimental import pallas as pl
from jax.experimental.pallas import tpu as pltpu
from jax.sharding import PartitionSpec as P

MESH = pl.DeviceIdType.MESH
F32 = jnp.float32
SLS = 3
STEPS = 8
RELAX = (0.6, 0.85, 0.97)
STEP_SQ = 0.25
RUN = 4
HALF = 8
EDGE = 8
SENT = 28
NOW, PREV, MEM, MOD, QW, ADJ = 0, 2, 4, 10, 11, 14


def snake(g, d):
    row, col = lax.div(d, RUN), lax.rem(d, RUN)
    flip = lax.rem(row + (g < HALF).astype(jnp.int32), 2) == 1
    return row * RUN + jnp.where(flip, RUN - 1 - col, col)


def kernel(
    groups,
    parts,
    up_h,
    un_h,
    mem_h,
    mod_h,
    q_h,
    adj_h,
    src_h,
    dst_h,
    wgt_h,
    o_u,
    o_mu,
    o_q,
    i0,
    isrc,
    idst,
    iwgt,
    flip,
    s_1,
    r_1,
    s_2,
    r_2,
    s_b,
    r_b,
    s_o,
    r_o,
    s_e,
    r_e,
    src,
    dst,
    wgt,
    mod0,
    q0,
    adj0,
    xp,
    vp,
    xold,
    vold,
    m0,
    p0,
    cx,
    cv,
    lap0,
    vel0,
    mem0,
    s_l,
    s_r,
    f_l,
    f_r,
    ext,
    zp,
    zold,
    p1,
    lap1,
    vel1,
    mem1,
    s_col,
    r_col,
    in_sem,
    bulk_send,
    bulk_recv,
    side_send,
    side_recv,
    col_send,
    col_recv,
    row_send,
    row_recv,
):
    g, d = lax.axis_index("group"), lax.axis_index("dom")
    last = parts - 1
    turned = lax.rem(g, 2) == 1

    def turn_pos(n):
        return jnp.where(turned, last - n, n)

    place = snake(g, d)
    pos = turn_pos(place)
    has_lo, has_hi = g > 0, g < groups - 1
    at_top, at_end = d > 0, d < last
    first, final = pos == 0, pos == last
    at_left = jnp.logical_or(jnp.logical_not(first), has_lo)
    at_right = jnp.logical_or(jnp.logical_not(final), has_hi)
    prev = snake(g, jnp.maximum(place - 1, 0))
    after = snake(g, jnp.minimum(place + 1, last))
    lo_g, hi_g = jnp.maximum(g - 1, 0), jnp.minimum(g + 1, groups - 1)
    left = (
        jnp.where(first, lo_g, g),
        jnp.where(first, snake(lo_g, place), jnp.where(turned, after, prev)),
    )
    right = (
        jnp.where(final, hi_g, g),
        jnp.where(final, snake(hi_g, place), jnp.where(turned, prev, after)),
    )
    over_lo = jnp.logical_and(first, g == HALF)
    over_hi = jnp.logical_and(jnp.logical_and(final, has_hi), g == HALF - 1)

    def far(t):
        half = lax.div(t + 1, 2)
        step = jnp.where(lax.rem(t, 2) == 1, half, -half)
        return lax.rem(d + parts // 2 + step, parts)

    barrier = pltpu.get_barrier_semaphore()

    def hello(group, part):
        pl.semaphore_signal(barrier, inc=1, device_id=(group, part), device_id_type=MESH)

    def greet(t, carry):
        hello(g, far(t))
        return carry

    beside = []
    for away, group_there in ((-1, has_lo), (1, has_hi)):
        for step, part_there in ((-1, at_top), (0, True), (1, at_end)):
            there = group_there if part_there is True else jnp.logical_and(group_there, part_there)
            beside.append((away, step, there))
    guests = last + over_lo.astype(jnp.int32) + over_hi.astype(jnp.int32)
    for away, step, there in beside:
        pl.when(there)(functools.partial(hello, g + away, d + step))
        guests = guests + there.astype(jnp.int32)
    pl.when(over_lo)(functools.partial(hello, *left))
    pl.when(over_hi)(functools.partial(hello, *right))
    lax.fori_loop(0, last, greet, 0)

    core = pl.ds(EDGE, 32)
    pairs = [
        (un_h.at[0], i0.at[0]),
        (adj_h.at[:, 0], i0.at[pl.ds(5, STEPS)]),
        (src_h, isrc),
        (dst_h, idst),
        (wgt_h, iwgt),
        (up_h.at[0], i0.at[1]),
        (mem_h.at[:, 0], i0.at[pl.ds(2, SLS)]),
        (mod_h, ext.at[0, MOD, core]),
        (q_h, ext.at[0, pl.ds(QW, SLS), core]),
        (un_h.at[pl.ds(1, 2)], ext.at[0, pl.ds(NOW, 2), core]),
        (up_h.at[pl.ds(1, 2)], ext.at[0, pl.ds(PREV, 2), core]),
    ]
    for l in range(SLS):
        pairs.append((mem_h.at[l, pl.ds(1, 2)], ext.at[0, pl.ds(MEM + 2 * l, 2), core]))
    for n in range(STEPS):
        spot = ADJ + 2 * (STEPS - 1 - n)
        pairs.append((adj_h.at[n, pl.ds(1, 2)], ext.at[0, pl.ds(spot, 2), core]))
    loads = []
    for at, (source, target) in enumerate(pairs):
        loads.append(pltpu.make_async_copy(source, target, in_sem.at[at]))
        loads[-1].start()

    def clear(ref, *at):
        def run():
            ref[at] = jnp.zeros_like(ref[at])

        return run

    no = jnp.logical_not
    pl.when(no(at_left))(clear(f_l, slice(None)))
    pl.when(no(at_right))(clear(f_r, slice(None)))
    pl.when(no(at_top))(clear(ext, 0, slice(0, SENT), slice(0, EDGE)))
    pl.when(no(at_end))(clear(ext, 0, slice(0, SENT), slice(EDGE + 32, 2 * EDGE + 32)))
    for away, step, there in beside:
        pl.when(no(there))(clear(r_col, (away + 1) // 2, step + 1))
    zp[...] = jnp.zeros_like(zp)
    zold[...] = jnp.zeros_like(zold)
    p1[...] = jnp.zeros_like(p1)

    lane = lax.broadcasted_iota(jnp.int32, (32, 128), 1)
    low = lane < 64
    edge = lax.broadcasted_iota(jnp.int32, (128, 128), 1)
    wide = edge < 64
    zero = jnp.zeros((32, 128), F32)

    for load in loads:
        load.wait()

    def pack4(planes, target, row):
        flip[...] = jnp.concatenate(planes, axis=0).T
        target[pl.ds(row, parts, stride=8), :] = flip[pl.ds(0, parts, stride=2), :]
        target[pl.ds(row + 1, parts, stride=8), :] = flip[pl.ds(1, parts, stride=2), :]

    flip[...] = jnp.concatenate([i0[0], i0[5 + STEPS - 1], zero, zero], axis=0).T
    s_1[pl.ds(0, parts, stride=8), :] = jnp.where(
        wide[0:64],
        flip[pl.ds(0, parts, stride=2), :],
        pltpu.roll(flip[pl.ds(1, parts, stride=2), :], 64, 1),
    )
    for t, table in enumerate((isrc, idst, iwgt)):
        row = jnp.concatenate([table[0:1, :].astype(F32), table[1:2, :].astype(F32)], axis=1)
        s_2[pl.ds(t, parts, stride=8), :] = jnp.broadcast_to(row, (parts, 128))
    pack4([i0[1], i0[2], i0[3], i0[4]], s_2, 3)
    pack4([ext[0, MOD, core], ext[0, QW, core], ext[0, QW + 1, core], ext[0, QW + 2, core]], s_2, 5)
    pack4([i0[5], i0[6], i0[7], i0[8]], s_b, 0)
    pack4([i0[9], i0[10], i0[11], i0[11]], s_b, 2)

    for t in range(SENT // 4):
        tile = ext[0, 4 * t : 4 * t + 4, core, :].reshape(128, 128).T
        s_col[0, t] = tile[0:EDGE]
        s_col[1, t] = tile[128 - EDGE :]

    pl.semaphore_wait(barrier, guests)

    def spread(source, target, rows, which, by_pos):
        def send(t, carry):
            peer = far(t)
            take = turn_pos(snake(g, peer)) if by_pos else peer
            land = d if by_pos else pos
            pltpu.make_async_remote_copy(
                src_ref=source.at[pl.ds(pl.multiple_of(take * 8, 8), rows), :],
                dst_ref=target.at[pl.ds(pl.multiple_of(land * 8, 8), rows), :],
                send_sem=bulk_send.at[which],
                recv_sem=bulk_recv.at[which],
                device_id=(g, peer),
                device_id_type=MESH,
            ).start()
            return carry

        lax.fori_loop(0, last, send, 0)
        mine = pl.ds(pl.multiple_of((pos if by_pos else d) * 8, 8), 8)
        here = pl.ds(pl.multiple_of((d if by_pos else pos) * 8, 8), 8)
        target[here, :] = source[mine, :]

    def bulk(source, target, rows, which):
        return pltpu.make_async_remote_copy(
            src_ref=source.at[pl.ds(0, last * rows), :],
            dst_ref=target.at[pl.ds(0, last * rows), :],
            send_sem=bulk_send.at[which],
            recv_sem=bulk_recv.at[which],
            device_id=(g, lax.rem(d + 1, parts)),
            device_id_type=MESH,
        )

    def start_all(copies):
        for cond, copy, _ in copies:
            pl.when(cond)(copy.start)

    def recv_all(copies):
        for _, copy, cond in copies:
            pl.when(cond)(copy.wait_recv)

    def sent_all(copies):
        for cond, copy, _ in copies:
            pl.when(cond)(copy.wait_send)

    halo1 = []
    for at, (away, step, there) in enumerate(beside):
        side, back = (away + 1) // 2, len(beside) - 1 - at
        halo1.append(
            (
                there,
                pltpu.make_async_remote_copy(
                    src_ref=s_col.at[side],
                    dst_ref=r_col.at[1 - side, 1 - step],
                    send_sem=col_send.at[at],
                    recv_sem=col_recv.at[back],
                    device_id=(g + away, d + step),
                    device_id_type=MESH,
                ),
                beside[back][2],
            )
        )
    planes = pl.ds(0, SENT)
    for at, (step, there, source, target, other) in enumerate(
        ((-1, at_top, EDGE, EDGE + 32, at_end), (1, at_end, 32, 0, at_top))
    ):
        halo1.append(
            (
                there,
                pltpu.make_async_remote_copy(
                    src_ref=ext.at[0, planes, pl.ds(source, EDGE)],
                    dst_ref=ext.at[0, planes, pl.ds(target, EDGE)],
                    send_sem=row_send.at[at],
                    recv_sem=row_recv.at[at],
                    device_id=(g, d + step),
                    device_id_type=MESH,
                ),
                other,
            )
        )

    spread(s_1, r_1, 1, 0, True)
    start_all(halo1)
    spread(s_2, r_2, 7, 1, True)
    spread(s_b, r_b, 4, 2, True)

    def unpack(source, first, second):
        return jnp.concatenate(
            [
                source[pl.ds(first, parts, stride=8), :],
                source[pl.ds(second, parts, stride=8), :],
            ],
            axis=0,
        ).T

    def halo0(slot):
        return (
            (
                at_left,
                pltpu.make_async_remote_copy(
                    src_ref=s_l.at[slot],
                    dst_ref=f_r.at[slot],
                    send_sem=side_send.at[slot, 0],
                    recv_sem=side_recv.at[slot, 1],
                    device_id=left,
                    device_id_type=MESH,
                ),
                at_right,
            ),
            (
                at_right,
                pltpu.make_async_remote_copy(
                    src_ref=s_r.at[slot],
                    dst_ref=f_l.at[slot],
                    send_sem=side_send.at[slot, 1],
                    recv_sem=side_recv.at[slot, 0],
                    device_id=right,
                    device_id_type=MESH,
                ),
                at_left,
            ),
        )

    def show(slot, x, v):
        s_l[slot] = jnp.where(low, x, pltpu.roll(v, 64, 1))
        s_r[slot] = jnp.where(low, pltpu.roll(x, 64, 1), v)
        start_all(halo0(slot))

    bulk(s_1, r_1, 1, 0).wait_recv()
    both = unpack(r_1, 0, 0)
    x = jnp.where(low, both[0:32], both[64:96])
    v = STEP_SQ * jnp.where(low, both[32:64], both[96:128])
    show(0, x, v)
    xp[8:40, :] = x
    vp[8:40, :] = v
    vel0[STEPS - 1] = v
    vold[...] = zero
    for l in range(SLS):
        p0[l] = zero

    recv_all(halo1)
    inner = lax.rem(lax.broadcasted_iota(jnp.int32, (EDGE, 128), 1), 32) < 16
    blank = jnp.zeros((128 - 2 * EDGE, 128), F32)

    def beside_planes(tiles):
        return jnp.concatenate([tiles[1], blank, tiles[0]], axis=0).T.reshape(4, 32, 128)

    for t in range(SENT // 4):
        four = slice(4 * t, 4 * t + 4)
        ext[1, four, core, :] = beside_planes([r_col[side, 1, t] for side in range(2)])
        ends = beside_planes(
            [jnp.where(inner, r_col[side, 2, t], r_col[side, 0, t]) for side in range(2)]
        )
        ext[1, four, 0:EDGE, :] = ends[:, 32 - EDGE :, :]
        ext[1, four, EDGE + 32 : 2 * EDGE + 32, :] = ends[:, 0:EDGE, :]
    sent_all(halo1)
    for c in range(2):
        for t in range(2):
            zp[c, t, 8:56, :] = ext[t, NOW + c]
            zp[c + 2, t, 8:56, :] = STEP_SQ * ext[t, ADJ + c]
            zold[c, t] = ext[t, PREV + c]
        vel1[STEPS, c] = STEP_SQ * ext[0, ADJ + c, core, :]

    rim = lax.broadcasted_iota(jnp.int32, (48, 128), 1)

    def around(f):
        main, side = zp[f, 0, 8:56, :], zp[f, 1, 8:56, :]
        lap = []
        ahead = [pltpu.roll(a, 127, 1) for a in (main, side)]
        behind = [pltpu.roll(a, 1, 1) for a in (main, side)]
        for t, centre in enumerate((main, side)):
            lap.append(
                zp[f, t, 9:57, :]
                + zp[f, t, 7:55, :]
                + jnp.where(rim == 127, ahead[1 - t], ahead[t])
                + jnp.where(rim == 0, behind[1 - t], behind[t])
                - 4.0 * centre
            )
        return (main, side), lap

    def round1(k, carry):
        n = STEPS - 2 - k
        source = ADJ + 2 * jnp.minimum(k + 1, STEPS - 1)
        for c in range(2):
            now, lap = around(c)
            lap1[k, c] = lap[0][8:40]
            for l in range(SLS):
                mem1[k, l, c] = ext[0, MEM + 2 * l + c, core, :]
            for t in range(2):
                kept = [ext[t, MEM + 2 * l + c] for l in range(SLS)]
                force = ext[t, MOD] * lap[t]
                accel = force - (kept[0] + kept[1] + kept[2])
                fresh = 2.0 * now[t] - zold[c, t] + STEP_SQ * accel
                for l in range(SLS):
                    ext[t, MEM + 2 * l + c] = RELAX[l] * kept[l] + ext[t, QW + l] * force
                zold[c, t] = now[t]
                zp[c, t, 8:56, :] = fresh
            now, lap = around(c + 2)
            for t in range(2):
                kept = [p1[l, c, t] for l in range(SLS)]
                force = ext[t, MOD] * lap[t]
                accel = force - (kept[0] + kept[1] + kept[2]) + ext[t, source + c]
                fresh = 2.0 * now[t] - zold[c + 2, t] + STEP_SQ * accel
                for l in range(SLS):
                    p1[l, c, t] = RELAX[l] * kept[l] + ext[t, QW + l] * force
                zold[c + 2, t] = now[t]
                zp[c + 2, t, 8:56, :] = fresh
                if t == 0:
                    vel1[n + 1, c] = fresh[8:40]
        return carry

    lax.fori_loop(0, STEPS, round1, 0)

    def terms(vel, lap, mem, count):
        mu = zero
        q = [zero] * SLS
        for n in range(count):
            mu = mu + vel(n) * lap(n)
            for l in range(SLS):
                q[l] = q[l] + vel(n) * mem(n, l)
        return mu, q

    mu_sum, q_sum = zero, [zero] * SLS
    for c in range(2):
        o_u[c + 1] = zp[c, 0, 16:48, :]
        mu, q = terms(
            lambda n: vel1[n + 1, c], lambda n: lap1[n, c], lambda n, l: mem1[n, l, c], STEPS
        )
        mu_sum = mu_sum + mu
        q_sum = [a + b for a, b in zip(q_sum, q)]
    o_mu[...] = mu_sum
    for l in range(SLS):
        o_q[l] = q_sum[l]

    bulk(s_2, r_2, 7, 1).wait_recv()
    four = unpack(r_2, 3, 4)
    xold[...] = four[0:32]
    for l in range(SLS):
        m0[l] = four[32 + 32 * l : 64 + 32 * l]
    four = unpack(r_2, 5, 6)
    mod0[...] = four[0:32]
    for l in range(SLS):
        q0[l] = four[32 + 32 * l : 64 + 32 * l]
    src[...] = unpack(r_2, 0, 0)
    dst[...] = unpack(r_2, 1, 1)
    wgt[...] = unpack(r_2, 2, 2)

    def swap(a):
        t = a.T
        top, bottom = t[0:64], t[64:128]
        half = wide[0:64]
        return jnp.concatenate(
            [
                jnp.where(half, top, pltpu.roll(bottom, 64, 1)),
                jnp.where(half, pltpu.roll(top, 64, 1), bottom),
            ],
            axis=0,
        )

    def pick(table, plane):
        rows = table[...]
        out = jnp.zeros((128, 128), F32)
        for r in range(32):
            out = jnp.where(rows == float(r), plane[8 + r : 9 + r, :], out)
        return out

    def drop(table, values, out):
        rows = table[...]
        for r in range(32):
            out[r : r + 1, :] = jnp.sum(
                jnp.where(rows == float(r), values, 0.0), axis=0, keepdims=True
            )

    part = lax.rem(lax.broadcasted_iota(jnp.int32, (1, 128), 1), 64)

    def rims(plane):
        plane[7:8, :] = jnp.where(part == 0, 0.0, pltpu.roll(plane[39:40, :], 1, 1))
        plane[40:41, :] = jnp.where(part == 63, 0.0, pltpu.roll(plane[8:9, :], 127, 1))

    def ready(now, old, kept, other, turned_now, plane):
        own = plane[9:41, :] + plane[7:39, :] + turned_now - 4.0 * now
        rest = 2.0 * now - old + STEP_SQ * (other - (kept[0] + kept[1] + kept[2]))
        return own, rest

    def round0(k, adjoint):
        slot = lax.rem(k, 2)
        copies = halo0(slot)
        drop(dst, swap(pick(src, xp)) * wgt[...], cx)
        rims(xp)
        x = xp[8:40, :]
        m = [m0[l] for l in range(SLS)]
        x_own, x_rest = ready(x, xold[...], m, cx[...], pltpu.roll(x, 64, 1), xp)
        if adjoint:
            drop(src, swap(pick(dst, vp) * wgt[...]), cv)
            rims(vp)

            @pl.when(k == 0)
            def _():
                bulk(s_b, r_b, 4, 2).wait_recv()
                four = unpack(r_b, 0, 1)
                for n in range(4):
                    adj0[n] = four[n * 32 : n * 32 + 32]
                four = unpack(r_b, 2, 3)
                for n in range(3):
                    adj0[n + 4] = four[n * 32 : n * 32 + 32]

            n = STEPS - 2 - k
            v = vp[8:40, :]
            p = [p0[l] for l in range(SLS)]
            v_own, v_rest = ready(v, vold[...], p, cv[...] + adj0[n], pltpu.roll(v, 64, 1), vp)
        recv_all(copies)
        from_l, from_r = f_l[slot], f_r[slot]
        lap = x_own + jnp.where(low, from_l, pltpu.roll(from_r, 64, 1))
        force = mod0[...] * lap
        fresh = x_rest + STEP_SQ * force
        if adjoint:
            v_force = mod0[...] * (v_own + jnp.where(low, pltpu.roll(from_l, 64, 1), from_r))
            v_fresh = v_rest + STEP_SQ * v_force
            show(1 - slot, fresh, v_fresh)
        lap0[k] = lap
        xold[...] = x
        xp[8:40, :] = fresh
        if adjoint:
            for l in range(SLS):
                mem0[k, l] = m[l]
                m0[l] = RELAX[l] * m[l] + q0[l] * force
                p0[l] = RELAX[l] * p[l] + q0[l] * v_force
            vold[...] = v
            vp[8:40, :] = v_fresh
            vel0[n] = v_fresh
        sent_all(copies)

    def step0(k, carry):
        round0(k, True)
        return carry

    lax.fori_loop(0, STEPS - 1, step0, 0)

    mu, _ = terms(lambda n: vel0[n], lambda n: lap0[n], lambda n, l: zero, STEPS - 1)
    q = [zero] * SLS
    for n in range(STEPS):
        for l in range(SLS):
            q[l] = q[l] + vel0[n] * (mem0[n, l] if n < STEPS - 1 else m0[l])
    turn = jnp.concatenate([mu] + q, axis=0).T
    s_o[pl.ds(0, parts, stride=8), :] = turn[0:64]
    s_o[pl.ds(1, parts, stride=8), :] = turn[64:128]
    spread(s_o, r_o, 2, 3, False)

    round0(STEPS - 1, False)

    turn = jnp.concatenate([xp[8:40, :], vel0[STEPS - 1] * lap0[STEPS - 1], zero, zero], axis=0).T
    s_e[pl.ds(0, parts, stride=8), :] = jnp.where(
        wide[0:64], turn[0:64], pltpu.roll(turn[64:128], 64, 1)
    )
    spread(s_e, r_e, 1, 4, False)

    bulk(s_o, r_o, 2, 3).wait_recv()
    flip[pl.ds(0, parts, stride=2), :] = r_o[pl.ds(0, parts, stride=8), :]
    flip[pl.ds(1, parts, stride=2), :] = r_o[pl.ds(1, parts, stride=8), :]
    four = flip[...].T
    scale = 1.0 / (3.0 * STEPS)
    mu = o_mu[...] + four[0:32]
    for l in range(SLS):
        o_q[l] = (o_q[l] + four[32 + 32 * l : 64 + 32 * l]) * scale
    bulk(s_e, r_e, 1, 4).wait_recv()
    ends = r_e[pl.ds(0, parts, stride=8), :]
    flip[pl.ds(0, parts, stride=2), :] = ends
    flip[pl.ds(1, parts, stride=2), :] = pltpu.roll(ends, 64, 1)
    four = flip[...].T
    o_u[0] = four[0:32]
    o_mu[...] = (mu + four[32:64]) * scale

    bulk(s_1, r_1, 1, 0).wait_send()
    bulk(s_2, r_2, 7, 1).wait_send()
    bulk(s_b, r_b, 4, 2).wait_send()
    bulk(s_o, r_o, 2, 3).wait_send()
    bulk(s_e, r_e, 1, 4).wait_send()


def solution(mesh):
    groups, parts = mesh.shape["group"], mesh.shape["dom"]

    def shards(
        u_prev, u_now, memory, modulus, q_weight, adjoint_source, couple_src, couple_dst, couple_weight
    ):
        tables = [t.reshape(parts, -1).T for t in (couple_src, couple_dst, couple_weight)]
        plane = (32, 128)
        square = (128, 128)

        def vmem(*shape):
            return pltpu.VMEM(shape, F32)

        dma = pltpu.SemaphoreType.DMA
        return pl.pallas_call(
            functools.partial(kernel, groups, parts),
            out_shape=(
                jax.ShapeDtypeStruct(u_now.shape, F32),
                jax.ShapeDtypeStruct(modulus.shape, F32),
                jax.ShapeDtypeStruct(q_weight.shape, F32),
            ),
            in_specs=[pl.BlockSpec(memory_space=pltpu.HBM)] * 9,
            out_specs=[pl.BlockSpec(memory_space=pltpu.VMEM)] * 3,
            scratch_shapes=[
                vmem(5 + STEPS, *plane),
                pltpu.VMEM((2, parts), jnp.int32),
                pltpu.VMEM((2, parts), jnp.int32),
                vmem(2, parts),
                vmem(*square),
            ]
            + [vmem(parts * 8, 128)] * 10
            + [
                vmem(*square),
                vmem(*square),
                vmem(*square),
                vmem(*plane),
                vmem(SLS, *plane),
                vmem(STEPS - 1, *plane),
                vmem(48, 128),
                vmem(48, 128),
                vmem(*plane),
                vmem(*plane),
                vmem(SLS, *plane),
                vmem(SLS, *plane),
                vmem(*plane),
                vmem(*plane),
                vmem(STEPS, *plane),
                vmem(STEPS, *plane),
                vmem(STEPS, SLS, *plane),
                vmem(2, *plane),
                vmem(2, *plane),
                vmem(2, *plane),
                vmem(2, *plane),
                vmem(2, SENT + 2, 48, 128),
                vmem(4, 2, 64, 128),
                vmem(4, 2, 48, 128),
                vmem(SLS, 2, 2, 48, 128),
                vmem(STEPS, 2, *plane),
                vmem(STEPS + 1, 2, *plane),
                vmem(STEPS, SLS, 2, *plane),
                vmem(2, SENT // 4, EDGE, 128),
                vmem(2, 3, SENT // 4, EDGE, 128),
                dma((22,)),
                dma((5,)),
                dma((5,)),
                dma((2, 2)),
                dma((2, 2)),
                dma((6,)),
                dma((6,)),
                dma((2,)),
                dma((2,)),
            ],
            compiler_params=pltpu.CompilerParams(
                collective_id=0, has_side_effects=True, vmem_limit_bytes=60 * 1024 * 1024
            ),
        )(u_prev, u_now, memory, modulus, q_weight, adjoint_source, *tables)

    in_specs = (
        P(None, "dom", "group"),
        P(None, "dom", "group"),
        P(None, None, "dom", "group"),
        P("dom", "group"),
        P(None, "dom", "group"),
        P(None, None, "dom", "group"),
        P("group", "dom", None, None),
        P("group", "dom", None, None),
        P("group", "dom", None, None),
    )
    out_specs = (P(None, "dom", "group"), P("dom", "group"), P(None, "dom", "group"))
    return jax.shard_map(shards, mesh=mesh, in_specs=in_specs, out_specs=out_specs, check_vma=False)
```

time: 670 us -> 87.1 us (0.13)
  starting transfers between devices: 449 us -> 0 us
  waiting for transfers between devices: 187 us -> 0 us
  Pallas kernels: 0 us -> 82.5 us
  local copies, waits for them, and re-layouts: 14.2 us -> 2.67 us
  matrix products: 8.46 us -> 0 us
    ppermute x64 -> x0, starting transfers between devices: 263 us -> none  [the longest x32 135 us: padded_2(): lax.ppermute(head, axis, [((i + 1) % count, i) for i in range(ends)])]
    all_to_all x16 -> x0, starting transfers between devices: 186 us -> none  [the longest x8 122 us: backward_couple(): lax.all_to_all(sent, 'dom', split_axis=0, concat_axis=0, tiled=True)]
    all_to_all x16 -> x0, waiting for transfers between devices: 117 us -> none  [the longest x8 100 us: forward_couple(): lax.all_to_all(sent, 'dom', split_axis=0, concat_axis=0, tiled=True)]
    pallas_call x0 -> x1, Pallas kernels: none -> 82.5 us  [shards(): pl.pallas_call(functools.partial(kernel, groups, parts), out_shape=(jax.S...]
    ppermute x64 -> x0, waiting for transfers between devices: 69.7 us -> none  [the longest x32 69.6 us: padded_2(): lax.ppermute(tail, axis, [(i, (i + 1) % count) for i in range(ends)])]
    dot_general x16 -> x0, local copies, waits for them, and re-layouts: 10.9 us -> none  [the longest x8 5.47 us: forward_couple(): jnp.dot(picker, radial, precision=lax.Precision.HIGHEST)]
    dot_general x32 -> x0, matrix products: 8.46 us -> none  [the longest x8 3.04 us: backward_couple(): jnp.dot(placer.T, radial, precision=lax.Precision.HIGHEST)]
  transfers between devices with their start and end apart: 80 -> 0, of which waited for: 26 -> 0; matrix products, arithmetic and copies ran while one was open for 3% -> 0% of each run, Pallas kernels for 0% -> 0%
where the time goes in v1:
time: 87.1 us; the launch traced here: 85.9 us
  Pallas kernels  82.5 us (95%)
  local copies, waits for them, and re-layouts  2.67 us (3%)
    pallas_call x1, Pallas kernels, shards(): pl.pallas_call(functools.partial(kernel, groups, parts), out_shape=(jax.S...  82.5 us
    unnamed x7, local copies, waits for them, and re-layouts  2.67 us

profile of v1, /device:TPU:56, one launch (start us, length us, event | category | flops | bytes accessed | tf_op | source)
XLA Modules:
  0.0 85.9 jit_solution(17358306033232910401)
XLA Ops:
  0.6 82.5 %shard_map.112 = (f32[3,32,128]{2,1,0:T(8,128)}, f32[32,128]{1,0:T(8,128)}, f32[3,32,128]{2,1,0:T(8,128)}) custom-call(f32[3,32,128]{2,1,0:T(8,128)} %up_h.1, f32[3,32,128]{2,1,0:T(8,128)} %un_h.1, f32[3,3,32,128]{3,2,1,0:T(8,128)} %mem_h.1, f32[32,128]{1,0:T(8,128)} %mod_h.1, f32[3,32,128]{2,1,0:T(8,128)} %q_h.1, f32[8,3,32,128]{3,2,1,0:T(8,128)} %adj_h.1, ...), custom_call_target="tpu_custom_call" | custom-call | tf_op jit(solution)/shard_map/pallas_call | solution.py:620
  83.2 0.0 copy-start.1
  83.2 0.0 copy-start
  83.2 1.4 %copy.15 = f32[3,32,128]{2,1,0:T(8,128)} copy(f32[3,32,128]{2,1,0:T(8,128)} %get-tuple-element.6) | data formatting | bytes 98304
  84.6 0.0 copy-done.1
  84.6 0.6 copy.16
  85.2 0.0 copy-done
  85.3 0.6 copy.17
Async XLA Ops:
  83.2 1.5 %copy-start.1 = (f32[32,128]{1,0:T(8,128)S(1)}, f32[32,128]{1,0:T(8,128)}, u32[]{:S(2)}) copy-start(f32[32,128]{1,0:T(8,128)} %get-tuple-element.7) | copy-start | bytes 49156
  83.2 2.1 %copy-start = (f32[3,32,128]{2,1,0:T(8,128)S(1)}, f32[3,32,128]{2,1,0:T(8,128)}, u32[]{:S(2)}) copy-start(f32[3,32,128]{2,1,0:T(8,128)} %get-tuple-element.8) | copy-start | bytes 147460

commit v2 on v1

--- a/solution.py
+++ b/solution.py
@@ -52,6 +52,9 @@
     r_2,
     s_b,
     r_b,
+    s_t,
+    r_t,
+    flat,
     s_o,
     r_o,
     s_e,
@@ -95,6 +98,8 @@
     col_recv,
     row_send,
     row_recv,
+    tab_send,
+    tab_recv,
 ):
     g, d = lax.axis_index("group"), lax.axis_index("dom")
     last = parts - 1
@@ -206,19 +211,24 @@
         target[pl.ds(row, parts, stride=8), :] = flip[pl.ds(0, parts, stride=2), :]
         target[pl.ds(row + 1, parts, stride=8), :] = flip[pl.ds(1, parts, stride=2), :]
 
-    flip[...] = jnp.concatenate([i0[0], i0[5 + STEPS - 1], zero, zero], axis=0).T
-    s_1[pl.ds(0, parts, stride=8), :] = jnp.where(
-        wide[0:64],
-        flip[pl.ds(0, parts, stride=2), :],
-        pltpu.roll(flip[pl.ds(1, parts, stride=2), :], 64, 1),
-    )
+    def pack2(planes, target, row):
+        flip[...] = jnp.concatenate(planes + [zero, zero], axis=0).T
+        target[pl.ds(row, parts, stride=8), :] = jnp.where(
+            wide[0:64],
+            flip[pl.ds(0, parts, stride=2), :],
+            pltpu.roll(flip[pl.ds(1, parts, stride=2), :], 64, 1),
+        )
+
+    adj = 5
+    pack2([i0[0], i0[adj + 7]], s_1, 0)
     for t, table in enumerate((isrc, idst, iwgt)):
         row = jnp.concatenate([table[0:1, :].astype(F32), table[1:2, :].astype(F32)], axis=1)
-        s_2[pl.ds(t, parts, stride=8), :] = jnp.broadcast_to(row, (parts, 128))
-    pack4([i0[1], i0[2], i0[3], i0[4]], s_2, 3)
-    pack4([ext[0, MOD, core], ext[0, QW, core], ext[0, QW + 1, core], ext[0, QW + 2, core]], s_2, 5)
-    pack4([i0[5], i0[6], i0[7], i0[8]], s_b, 0)
-    pack4([i0[9], i0[10], i0[11], i0[11]], s_b, 2)
+        s_t[t : t + 1, :] = row
+    pack4([i0[1], i0[2], i0[3], i0[4]], s_2, 0)
+    pack4([ext[0, MOD, core], ext[0, QW, core], ext[0, QW + 1, core], ext[0, QW + 2, core]], s_2, 2)
+    pack2([i0[adj + 6], i0[adj + 5]], s_2, 4)
+    pack4([i0[adj + 4], i0[adj + 3], i0[adj + 2], i0[adj + 1]], s_b, 0)
+    pack2([i0[adj], zero], s_b, 2)
 
     for t in range(SENT // 4):
         tile = ext[0, 4 * t : 4 * t + 4, core, :].reshape(128, 128).T
@@ -305,10 +315,49 @@
             )
         )
 
+    lines, depth = parts // RUN, 3
+    line, spot = lax.div(d, RUN), lax.rem(d, RUN)
+    slab = pl.ds(pl.multiple_of(spot * 8, 8), depth)
+
+    def along(t, carry):
+        half = lax.div(t + 1, 2)
+        step = jnp.where(lax.rem(t, 2) == 1, half, -half)
+        peer = lax.rem(line + lines // 2 + step, lines)
+        pltpu.make_async_remote_copy(
+            src_ref=s_t.at[pl.ds(0, depth)],
+            dst_ref=r_t.at[line, slab],
+            send_sem=tab_send.at[0],
+            recv_sem=tab_recv.at[0],
+            device_id=(g, peer * RUN + spot),
+            device_id_type=MESH,
+        ).start()
+        return carry
+
+    across = [
+        pltpu.make_async_remote_copy(
+            src_ref=r_t.at[:, slab],
+            dst_ref=r_t.at[:, slab],
+            send_sem=tab_send.at[step],
+            recv_sem=tab_recv.at[step],
+            device_id=(g, line * RUN + lax.rem(spot + step, RUN)),
+            device_id_type=MESH,
+        )
+        for step in range(1, RUN)
+    ]
+    tables = pltpu.make_async_remote_copy(
+        src_ref=r_t.at[pl.ds(0, lines - 1), pl.ds(0, depth)],
+        dst_ref=r_t.at[pl.ds(0, lines - 1), pl.ds(0, depth)],
+        send_sem=tab_send.at[0],
+        recv_sem=tab_recv.at[0],
+        device_id=(g, lax.rem(d + 1, parts)),
+        device_id_type=MESH,
+    )
+
+    lax.fori_loop(0, lines - 1, along, 0)
+    r_t[line, slab, :] = s_t[0:depth, :]
     spread(s_1, r_1, 1, 0, True)
-    start_all(halo1)
-    spread(s_2, r_2, 7, 1, True)
-    spread(s_b, r_b, 4, 2, True)
+    spread(s_2, r_2, 5, 1, True)
+    spread(s_b, r_b, 3, 2, True)
 
     def unpack(source, first, second):
         return jnp.concatenate(
@@ -352,10 +401,16 @@
         s_r[slot] = jnp.where(low, pltpu.roll(x, 64, 1), v)
         start_all(halo0(slot))
 
+    def unpack2(source, row):
+        both = unpack(source, row, row)
+        return [jnp.where(low, both[at : at + 32], both[at + 64 : at + 96]) for at in (0, 32)]
+
+    tables.wait_recv()
+    for copy in across:
+        copy.start()
     bulk(s_1, r_1, 1, 0).wait_recv()
-    both = unpack(r_1, 0, 0)
-    x = jnp.where(low, both[0:32], both[64:96])
-    v = STEP_SQ * jnp.where(low, both[32:64], both[96:128])
+    x, v = unpack2(r_1, 0)
+    v = STEP_SQ * v
     show(0, x, v)
     xp[8:40, :] = x
     vp[8:40, :] = v
@@ -363,6 +418,143 @@
     vold[...] = zero
     for l in range(SLS):
         p0[l] = zero
+
+    for copy in across:
+        copy.wait()
+    flat[...] = r_t[...].reshape(parts * 8, 128)
+    src[...] = unpack(flat, 0, 0)
+    dst[...] = unpack(flat, 1, 1)
+    wgt[...] = unpack(flat, 2, 2)
+    bulk(s_2, r_2, 5, 1).wait_recv()
+    four = unpack(r_2, 0, 1)
+    xold[...] = four[0:32]
+    for l in range(SLS):
+        m0[l] = four[32 + 32 * l : 64 + 32 * l]
+    four = unpack(r_2, 2, 3)
+    mod0[...] = four[0:32]
+    for l in range(SLS):
+        q0[l] = four[32 + 32 * l : 64 + 32 * l]
+    adj0[6], adj0[5] = unpack2(r_2, 4)
+
+    def swap(a):
+        t = a.T
+        top, bottom = t[0:64], t[64:128]
+        half = wide[0:64]
+        return jnp.concatenate(
+            [
+                jnp.where(half, top, pltpu.roll(bottom, 64, 1)),
+                jnp.where(half, pltpu.roll(top, 64, 1), bottom),
+            ],
+            axis=0,
+        )
+
+    def pick(table, plane):
+        rows = table[...]
+        out = jnp.zeros((128, 128), F32)
+        for r in range(32):
+            out = jnp.where(rows == float(r), plane[8 + r : 9 + r, :], out)
+        return out
+
+    def drop(table, values, out):
+        rows = table[...]
+        for r in range(32):
+            out[r : r + 1, :] = jnp.sum(
+                jnp.where(rows == float(r), values, 0.0), axis=0, keepdims=True
+            )
+
+    part = lax.rem(lax.broadcasted_iota(jnp.int32, (1, 128), 1), 64)
+
+    def rims(plane):
+        plane[7:8, :] = jnp.where(part == 0, 0.0, pltpu.roll(plane[39:40, :], 1, 1))
+        plane[40:41, :] = jnp.where(part == 63, 0.0, pltpu.roll(plane[8:9, :], 127, 1))
+
+    def ready(now, old, kept, other, turned_now, plane):
+        own = plane[9:41, :] + plane[7:39, :] + turned_now - 4.0 * now
+        rest = 2.0 * now - old + STEP_SQ * (other - (kept[0] + kept[1] + kept[2]))
+        return own, rest
+
+    def round0(k, adjoint):
+        slot = lax.rem(k, 2)
+        copies = halo0(slot)
+        drop(dst, swap(pick(src, xp)) * wgt[...], cx)
+        rims(xp)
+        x = xp[8:40, :]
+        m = [m0[l] for l in range(SLS)]
+        x_own, x_rest = ready(x, xold[...], m, cx[...], pltpu.roll(x, 64, 1), xp)
+        if adjoint:
+            drop(src, swap(pick(dst, vp) * wgt[...]), cv)
+            rims(vp)
+
+            @pl.when(k == 2)
+            def _():
+                bulk(s_b, r_b, 3, 2).wait_recv()
+                four = unpack(r_b, 0, 1)
+                for n in range(4):
+                    adj0[4 - n] = four[n * 32 : n * 32 + 32]
+                adj0[0] = unpack2(r_b, 2)[0]
+
+            n = STEPS - 2 - k
+            v = vp[8:40, :]
+            p = [p0[l] for l in range(SLS)]
+            v_own, v_rest = ready(v, vold[...], p, cv[...] + adj0[n], pltpu.roll(v, 64, 1), vp)
+        recv_all(copies)
+        from_l, from_r = f_l[slot], f_r[slot]
+        lap = x_own + jnp.where(low, from_l, pltpu.roll(from_r, 64, 1))
+        force = mod0[...] * lap
+        fresh = x_rest + STEP_SQ * force
+        if adjoint:
+            v_force = mod0[...] * (v_own + jnp.where(low, pltpu.roll(from_l, 64, 1), from_r))
+            v_fresh = v_rest + STEP_SQ * v_force
+            show(1 - slot, fresh, v_fresh)
+        lap0[k] = lap
+        xold[...] = x
+        xp[8:40, :] = fresh
+        if adjoint:
+            for l in range(SLS):
+                mem0[k, l] = m[l]
+                m0[l] = RELAX[l] * m[l] + q0[l] * force
+                p0[l] = RELAX[l] * p[l] + q0[l] * v_force
+            vold[...] = v
+            vp[8:40, :] = v_fresh
+            vel0[n] = v_fresh
+        sent_all(copies)
+
+    def step0(k, carry):
+        @pl.when(k == 3)
+        def _():
+            start_all(halo1)
+
+        round0(k, True)
+        return carry
+
+    lax.fori_loop(0, STEPS - 1, step0, 0)
+
+    def terms(vel, lap, mem, count):
+        mu = zero
+        q = [zero] * SLS
+        for n in range(count):
+            mu = mu + vel(n) * lap(n)
+            for l in range(SLS):
+                q[l] = q[l] + vel(n) * mem(n, l)
+        return mu, q
+
+    mu, _ = terms(lambda n: vel0[n], lambda n: lap0[n], lambda n, l: zero, STEPS - 1)
+    q = [zero] * SLS
+    for n in range(STEPS):
+        for l in range(SLS):
+            q[l] = q[l] + vel0[n] * (mem0[n, l] if n < STEPS - 1 else m0[l])
+    turn = jnp.concatenate([mu] + q, axis=0).T
+    s_o[pl.ds(0, parts, stride=8), :] = turn[0:64]
+    s_o[pl.ds(1, parts, stride=8), :] = turn[64:128]
+    spread(s_o, r_o, 2, 3, False)
+
+    round0(STEPS - 1, False)
+
+    turn = jnp.concatenate([xp[8:40, :], vel0[STEPS - 1] * lap0[STEPS - 1], zero, zero], axis=0).T
+    s_e[pl.ds(0, parts, stride=8), :] = jnp.where(
+        wide[0:64], turn[0:64], pltpu.roll(turn[64:128], 64, 1)
+    )
+    spread(s_e, r_e, 1, 4, False)
 
     recv_all(halo1)
     inner = lax.rem(lax.broadcasted_iota(jnp.int32, (EDGE, 128), 1), 32) < 16
@@ -437,15 +629,6 @@
 
     lax.fori_loop(0, STEPS, round1, 0)
 
-    def terms(vel, lap, mem, count):
-        mu = zero
-        q = [zero] * SLS
-        for n in range(count):
-            mu = mu + vel(n) * lap(n)
-            for l in range(SLS):
-                q[l] = q[l] + vel(n) * mem(n, l)
-        return mu, q
-
     mu_sum, q_sum = zero, [zero] * SLS
     for c in range(2):
         o_u[c + 1] = zp[c, 0, 16:48, :]
@@ -457,128 +640,6 @@
     o_mu[...] = mu_sum
     for l in range(SLS):
         o_q[l] = q_sum[l]
-
-    bulk(s_2, r_2, 7, 1).wait_recv()
-    four = unpack(r_2, 3, 4)
-    xold[...] = four[0:32]
-    for l in range(SLS):
-        m0[l] = four[32 + 32 * l : 64 + 32 * l]
-    four = unpack(r_2, 5, 6)
-    mod0[...] = four[0:32]
-    for l in range(SLS):
-        q0[l] = four[32 + 32 * l : 64 + 32 * l]
-    src[...] = unpack(r_2, 0, 0)
-    dst[...] = unpack(r_2, 1, 1)
-    wgt[...] = unpack(r_2, 2, 2)
-
-    def swap(a):
-        t = a.T
-        top, bottom = t[0:64], t[64:128]
-        half = wide[0:64]
-        return jnp.concatenate(
-            [
-                jnp.where(half, top, pltpu.roll(bottom, 64, 1)),
-                jnp.where(half, pltpu.roll(top, 64, 1), bottom),
-            ],
-            axis=0,
-        )
-
-    def pick(table, plane):
-        rows = table[...]
-        out = jnp.zeros((128, 128), F32)
-        for r in range(32):
-            out = jnp.where(rows == float(r), plane[8 + r : 9 + r, :], out)
-        return out
-
-    def drop(table, values, out):
-        rows = table[...]
-        for r in range(32):
-            out[r : r + 1, :] = jnp.sum(
-                jnp.where(rows == float(r), values, 0.0), axis=0, keepdims=True
-            )
-
-    part = lax.rem(lax.broadcasted_iota(jnp.int32, (1, 128), 1), 64)
-
-    def rims(plane):
-        plane[7:8, :] = jnp.where(part == 0, 0.0, pltpu.roll(plane[39:40, :], 1, 1))
-        plane[40:41, :] = jnp.where(part == 63, 0.0, pltpu.roll(plane[8:9, :], 127, 1))
-
-    def ready(now, old, kept, other, turned_now, plane):
-        own = plane[9:41, :] + plane[7:39, :] + turned_now - 4.0 * now
-        rest = 2.0 * now - old + STEP_SQ * (other - (kept[0] + kept[1] + kept[2]))
-        return own, rest
-
-    def round0(k, adjoint):
-        slot = lax.rem(k, 2)
-        copies = halo0(slot)
-        drop(dst, swap(pick(src, xp)) * wgt[...], cx)
-        rims(xp)
-        x = xp[8:40, :]
-        m = [m0[l] for l in range(SLS)]
-        x_own, x_rest = ready(x, xold[...], m, cx[...], pltpu.roll(x, 64, 1), xp)
-        if adjoint:
-            drop(src, swap(pick(dst, vp) * wgt[...]), cv)
-            rims(vp)
-
-            @pl.when(k == 0)
-            def _():
-                bulk(s_b, r_b, 4, 2).wait_recv()
-                four = unpack(r_b, 0, 1)
-                for n in range(4):
-                    adj0[n] = four[n * 32 : n * 32 + 32]
-                four = unpack(r_b, 2, 3)
-                for n in range(3):
-                    adj0[n + 4] = four[n * 32 : n * 32 + 32]
-
-            n = STEPS - 2 - k
-            v = vp[8:40, :]
-            p = [p0[l] for l in range(SLS)]
-            v_own, v_rest = ready(v, vold[...], p, cv[...] + adj0[n], pltpu.roll(v, 64, 1), vp)
-        recv_all(copies)
-        from_l, from_r = f_l[slot], f_r[slot]
-        lap = x_own + jnp.where(low, from_l, pltpu.roll(from_r, 64, 1))
-        force = mod0[...] * lap
-        fresh = x_rest + STEP_SQ * force
-        if adjoint:
-            v_force = mod0[...] * (v_own + jnp.where(low, pltpu.roll(from_l, 64, 1), from_r))
-            v_fresh = v_rest + STEP_SQ * v_force
-            show(1 - slot, fresh, v_fresh)
-        lap0[k] = lap
-        xold[...] = x
-        xp[8:40, :] = fresh
-        if adjoint:
-            for l in range(SLS):
-                mem0[k, l] = m[l]
-                m0[l] = RELAX[l] * m[l] + q0[l] * force
-                p0[l] = RELAX[l] * p[l] + q0[l] * v_force
-            vold[...] = v
-            vp[8:40, :] = v_fresh
-            vel0[n] = v_fresh
-        sent_all(copies)
-
-    def step0(k, carry):
-        round0(k, True)
-        return carry
-
-    lax.fori_loop(0, STEPS - 1, step0, 0)
-
-    mu, _ = terms(lambda n: vel0[n], lambda n: lap0[n], lambda n, l: zero, STEPS - 1)
-    q = [zero] * SLS
-    for n in range(STEPS):
-        for l in range(SLS):
-            q[l] = q[l] + vel0[n] * (mem0[n, l] if n < STEPS - 1 else m0[l])
-    turn = jnp.concatenate([mu] + q, axis=0).T
-    s_o[pl.ds(0, parts, stride=8), :] = turn[0:64]
-    s_o[pl.ds(1, parts, stride=8), :] = turn[64:128]
-    spread(s_o, r_o, 2, 3, False)
-
-    round0(STEPS - 1, False)
-
-    turn = jnp.concatenate([xp[8:40, :], vel0[STEPS - 1] * lap0[STEPS - 1], zero, zero], axis=0).T
-    s_e[pl.ds(0, parts, stride=8), :] = jnp.where(
-        wide[0:64], turn[0:64], pltpu.roll(turn[64:128], 64, 1)
-    )
-    spread(s_e, r_e, 1, 4, False)
 
     bulk(s_o, r_o, 2, 3).wait_recv()
     flip[pl.ds(0, parts, stride=2), :] = r_o[pl.ds(0, parts, stride=8), :]
@@ -597,8 +658,9 @@
     o_mu[...] = (mu + four[32:64]) * scale
 
     bulk(s_1, r_1, 1, 0).wait_send()
-    bulk(s_2, r_2, 7, 1).wait_send()
-    bulk(s_b, r_b, 4, 2).wait_send()
+    bulk(s_2, r_2, 5, 1).wait_send()
+    bulk(s_b, r_b, 3, 2).wait_send()
+    tables.wait_send()
     bulk(s_o, r_o, 2, 3).wait_send()
     bulk(s_e, r_e, 1, 4).wait_send()
 
@@ -619,11 +681,7 @@
         dma = pltpu.SemaphoreType.DMA
         return pl.pallas_call(
             functools.partial(kernel, groups, parts),
-            out_shape=(
-                jax.ShapeDtypeStruct(u_now.shape, F32),
-                jax.ShapeDtypeStruct(modulus.shape, F32),
-                jax.ShapeDtypeStruct(q_weight.shape, F32),
-            ),
+            out_shape=(vmem(*u_now.shape), vmem(*modulus.shape), vmem(*q_weight.shape)),
             in_specs=[pl.BlockSpec(memory_space=pltpu.HBM)] * 9,
             out_specs=[pl.BlockSpec(memory_space=pltpu.VMEM)] * 3,
             scratch_shapes=[
@@ -633,7 +691,9 @@
                 vmem(2, parts),
                 vmem(*square),
             ]
-            + [vmem(parts * 8, 128)] * 10
+            + [vmem(parts * 8, 128)] * 6
+            + [vmem(8, 128), vmem(parts // RUN, RUN * 8, 128)]
+            + [vmem(parts * 8, 128)] * 5
             + [
                 vmem(*square),
                 vmem(*square),
@@ -674,6 +734,8 @@
                 dma((6,)),
                 dma((2,)),
                 dma((2,)),
+                dma((RUN,)),
+                dma((RUN,)),
             ],
             compiler_params=pltpu.CompilerParams(
                 collective_id=0, has_side_effects=True, vmem_limit_bytes=60 * 1024 * 1024

time: 87.1 us -> 77.1 us (0.89)
  Pallas kernels: 82.5 us -> 74.1 us
    pallas_call x1, Pallas kernels: 82.5 us -> 74.1 us  [shards(): pl.pallas_call(functools.partial(kernel, groups, parts), out_shape=(vmem(...]
    unnamed x7 -> x3, local copies, waits for them, and re-layouts: 2.67 us -> 1.85 us
where the time goes in v2:
time: 77.1 us; the launch traced here: 76.6 us
  Pallas kernels  74.1 us (96%)
  local copies, waits for them, and re-layouts  1.85 us (2%)
    pallas_call x1, Pallas kernels, shards(): pl.pallas_call(functools.partial(kernel, groups, parts), out_shape=(vmem(...  74.1 us
    unnamed x3, local copies, waits for them, and re-layouts  1.85 us

profile of v2, /device:TPU:56, one launch (start us, length us, event | category | flops | bytes accessed | tf_op | source)
XLA Modules:
  0.0 76.6 jit_solution(3587428471044234140)
XLA Ops:
  0.6 74.1 %shard_map.112 = (f32[3,32,128]{2,1,0:T(8,128)S(1)}, f32[32,128]{1,0:T(8,128)S(1)}, f32[3,32,128]{2,1,0:T(8,128)S(1)}) custom-call(f32[3,32,128]{2,1,0:T(8,128)} %up_h.1, f32[3,32,128]{2,1,0:T(8,128)} %un_h.1, f32[3,3,32,128]{3,2,1,0:T(8,128)} %mem_h.1, f32[32,128]{1,0:T(8,128)} %mod_h.1, f32[3,32,128]{2,1,0:T(8,128)} %q_h.1, f32[8,3,32,128]{3,2,1,0:T(8,128)} %adj_h.1, ...), custom_call_target="tpu_custom_call" | custom-call | tf_op jit(solution)/shard_map/pallas_call | solution.py:682
  74.8 0.6 copy.15
  75.4 0.6 copy.16
  76.0 0.6 copy.17

commit v3 on v2

--- a/solution.py
+++ b/solution.py
@@ -52,6 +52,8 @@
     r_2,
     s_b,
     r_b,
+    s_q,
+    r_q,
     s_t,
     r_t,
     flat,
@@ -73,6 +75,8 @@
     p0,
     cx,
     cv,
+    fx,
+    fv,
     lap0,
     vel0,
     mem0,
@@ -225,8 +229,8 @@
         row = jnp.concatenate([table[0:1, :].astype(F32), table[1:2, :].astype(F32)], axis=1)
         s_t[t : t + 1, :] = row
     pack4([i0[1], i0[2], i0[3], i0[4]], s_2, 0)
-    pack4([ext[0, MOD, core], ext[0, QW, core], ext[0, QW + 1, core], ext[0, QW + 2, core]], s_2, 2)
-    pack2([i0[adj + 6], i0[adj + 5]], s_2, 4)
+    pack2([ext[0, MOD, core], i0[adj + 6]], s_2, 2)
+    pack4([ext[0, QW, core], ext[0, QW + 1, core], ext[0, QW + 2, core], i0[adj + 5]], s_q, 0)
     pack4([i0[adj + 4], i0[adj + 3], i0[adj + 2], i0[adj + 1]], s_b, 0)
     pack2([i0[adj], zero], s_b, 2)
 
@@ -356,7 +360,8 @@
     lax.fori_loop(0, lines - 1, along, 0)
     r_t[line, slab, :] = s_t[0:depth, :]
     spread(s_1, r_1, 1, 0, True)
-    spread(s_2, r_2, 5, 1, True)
+    spread(s_2, r_2, 3, 1, True)
+    spread(s_q, r_q, 2, 5, True)
     spread(s_b, r_b, 3, 2, True)
 
     def unpack(source, first, second):
@@ -425,16 +430,12 @@
     src[...] = unpack(flat, 0, 0)
     dst[...] = unpack(flat, 1, 1)
     wgt[...] = unpack(flat, 2, 2)
-    bulk(s_2, r_2, 5, 1).wait_recv()
+    bulk(s_2, r_2, 3, 1).wait_recv()
     four = unpack(r_2, 0, 1)
     xold[...] = four[0:32]
     for l in range(SLS):
         m0[l] = four[32 + 32 * l : 64 + 32 * l]
-    four = unpack(r_2, 2, 3)
-    mod0[...] = four[0:32]
-    for l in range(SLS):
-        q0[l] = four[32 + 32 * l : 64 + 32 * l]
-    adj0[6], adj0[5] = unpack2(r_2, 4)
+    mod0[...], adj0[6] = unpack2(r_2, 2)
 
     def swap(a):
         t = a.T
@@ -473,17 +474,39 @@
         rest = 2.0 * now - old + STEP_SQ * (other - (kept[0] + kept[1] + kept[2]))
         return own, rest
 
+    def absorb(k, adjoint):
+        for l in range(SLS):
+            mem0[k - 1, l] = m0[l]
+            m0[l] = RELAX[l] * m0[l] + q0[l] * fx[...]
+            if adjoint:
+                p0[l] = RELAX[l] * p0[l] + q0[l] * fv[...]
+
     def round0(k, adjoint):
         slot = lax.rem(k, 2)
         copies = halo0(slot)
         drop(dst, swap(pick(src, xp)) * wgt[...], cx)
         rims(xp)
+        if adjoint:
+            drop(src, swap(pick(dst, vp) * wgt[...]), cv)
+            rims(vp)
+        if adjoint:
+
+            @pl.when(k == 1)
+            def _():
+                bulk(s_q, r_q, 2, 5).wait_recv()
+                four = unpack(r_q, 0, 1)
+                for l in range(SLS):
+                    q0[l] = four[32 * l : 32 * l + 32]
+                adj0[5] = four[96:128]
+
+            @pl.when(k > 0)
+            def _():
+                absorb(k, True)
+
         x = xp[8:40, :]
         m = [m0[l] for l in range(SLS)]
         x_own, x_rest = ready(x, xold[...], m, cx[...], pltpu.roll(x, 64, 1), xp)
         if adjoint:
-            drop(src, swap(pick(dst, vp) * wgt[...]), cv)
-            rims(vp)
 
             @pl.when(k == 2)
             def _():
@@ -510,17 +533,15 @@
         xold[...] = x
         xp[8:40, :] = fresh
         if adjoint:
-            for l in range(SLS):
-                mem0[k, l] = m[l]
-                m0[l] = RELAX[l] * m[l] + q0[l] * force
-                p0[l] = RELAX[l] * p[l] + q0[l] * v_force
+            fx[...] = force
+            fv[...] = v_force
             vold[...] = v
             vp[8:40, :] = v_fresh
             vel0[n] = v_fresh
         sent_all(copies)
 
     def step0(k, carry):
-        @pl.when(k == 3)
+        @pl.when(k == 4)
         def _():
             start_all(halo1)
 
@@ -528,6 +549,7 @@
         return carry
 
     lax.fori_loop(0, STEPS - 1, step0, 0)
+    absorb(STEPS - 1, False)
 
     def terms(vel, lap, mem, count):
         mu = zero
@@ -658,7 +680,8 @@
     o_mu[...] = (mu + four[32:64]) * scale
 
     bulk(s_1, r_1, 1, 0).wait_send()
-    bulk(s_2, r_2, 5, 1).wait_send()
+    bulk(s_2, r_2, 3, 1).wait_send()
+    bulk(s_q, r_q, 2, 5).wait_send()
     bulk(s_b, r_b, 3, 2).wait_send()
     tables.wait_send()
     bulk(s_o, r_o, 2, 3).wait_send()
@@ -691,7 +714,7 @@
                 vmem(2, parts),
                 vmem(*square),
             ]
-            + [vmem(parts * 8, 128)] * 6
+            + [vmem(parts * 8, 128)] * 8
             + [vmem(8, 128), vmem(parts // RUN, RUN * 8, 128)]
             + [vmem(parts * 8, 128)] * 5
             + [
@@ -707,6 +730,8 @@
                 vmem(*plane),
                 vmem(SLS, *plane),
                 vmem(SLS, *plane),
+                vmem(*plane),
+                vmem(*plane),
                 vmem(*plane),
                 vmem(*plane),
                 vmem(STEPS, *plane),
@@ -726,8 +751,8 @@
                 vmem(2, SENT // 4, EDGE, 128),
                 vmem(2, 3, SENT // 4, EDGE, 128),
                 dma((22,)),
-                dma((5,)),
-                dma((5,)),
+                dma((6,)),
+                dma((6,)),
                 dma((2, 2)),
                 dma((2, 2)),
                 dma((6,)),

time: 77.1 us -> 76.4 us (level)
  Pallas kernels: 74.1 us -> 73.2 us
    pallas_call x1, Pallas kernels: 74.1 us -> 73.2 us  [shards(): pl.pallas_call(functools.partial(kernel, groups, parts), out_shape=(vmem(...]
where the time goes in v3:
time: 76.4 us; the launch traced here: 75.7 us
  Pallas kernels  73.2 us (96%)
  local copies, waits for them, and re-layouts  1.85 us (2%)
    pallas_call x1, Pallas kernels, shards(): pl.pallas_call(functools.partial(kernel, groups, parts), out_shape=(vmem(...  73.2 us
    unnamed x3, local copies, waits for them, and re-layouts  1.85 us

profile of v3, /device:TPU:56, one launch (start us, length us, event | category | flops | bytes accessed | tf_op | source)
XLA Modules:
  0.0 75.7 jit_solution(3701547210877796682)
XLA Ops:
  0.6 73.2 %shard_map.112 = (f32[3,32,128]{2,1,0:T(8,128)S(1)}, f32[32,128]{1,0:T(8,128)S(1)}, f32[3,32,128]{2,1,0:T(8,128)S(1)}) custom-call(f32[3,32,128]{2,1,0:T(8,128)} %up_h.1, f32[3,32,128]{2,1,0:T(8,128)} %un_h.1, f32[3,3,32,128]{3,2,1,0:T(8,128)} %mem_h.1, f32[32,128]{1,0:T(8,128)} %mod_h.1, f32[3,32,128]{2,1,0:T(8,128)} %q_h.1, f32[8,3,32,128]{3,2,1,0:T(8,128)} %adj_h.1, ...), custom_call_target="tpu_custom_call" | custom-call | tf_op jit(solution)/shard_map/pallas_call | solution.py:705
  73.9 0.6 copy.15
  74.5 0.6 copy.16
  75.1 0.6 copy.17

commit v4 on v3

--- a/solution.py
+++ b/solution.py
@@ -54,6 +54,8 @@
     r_b,
     s_q,
     r_q,
+    s_c,
+    r_c,
     s_t,
     r_t,
     flat,
@@ -231,8 +233,9 @@
     pack4([i0[1], i0[2], i0[3], i0[4]], s_2, 0)
     pack2([ext[0, MOD, core], i0[adj + 6]], s_2, 2)
     pack4([ext[0, QW, core], ext[0, QW + 1, core], ext[0, QW + 2, core], i0[adj + 5]], s_q, 0)
-    pack4([i0[adj + 4], i0[adj + 3], i0[adj + 2], i0[adj + 1]], s_b, 0)
-    pack2([i0[adj], zero], s_b, 2)
+    pack2([i0[adj + 4], i0[adj + 3]], s_b, 0)
+    pack2([i0[adj + 2], i0[adj + 1]], s_c, 0)
+    pack2([i0[adj], zero], s_c, 1)
 
     for t in range(SENT // 4):
         tile = ext[0, 4 * t : 4 * t + 4, core, :].reshape(128, 128).T
@@ -362,7 +365,7 @@
     spread(s_1, r_1, 1, 0, True)
     spread(s_2, r_2, 3, 1, True)
     spread(s_q, r_q, 2, 5, True)
-    spread(s_b, r_b, 3, 2, True)
+    spread(s_b, r_b, 1, 2, True)
 
     def unpack(source, first, second):
         return jnp.concatenate(
@@ -510,11 +513,14 @@
 
             @pl.when(k == 2)
             def _():
-                bulk(s_b, r_b, 3, 2).wait_recv()
-                four = unpack(r_b, 0, 1)
-                for n in range(4):
-                    adj0[4 - n] = four[n * 32 : n * 32 + 32]
-                adj0[0] = unpack2(r_b, 2)[0]
+                bulk(s_b, r_b, 1, 2).wait_recv()
+                adj0[4], adj0[3] = unpack2(r_b, 0)
+
+            @pl.when(k == 4)
+            def _():
+                bulk(s_c, r_c, 2, 6).wait_recv()
+                adj0[2], adj0[1] = unpack2(r_c, 0)
+                adj0[0] = unpack2(r_c, 1)[0]
 
             n = STEPS - 2 - k
             v = vp[8:40, :]
@@ -541,6 +547,10 @@
         sent_all(copies)
 
     def step0(k, carry):
+        @pl.when(k == 1)
+        def _():
+            spread(s_c, r_c, 2, 6, True)
+
         @pl.when(k == 4)
         def _():
             start_all(halo1)
@@ -682,7 +692,8 @@
     bulk(s_1, r_1, 1, 0).wait_send()
     bulk(s_2, r_2, 3, 1).wait_send()
     bulk(s_q, r_q, 2, 5).wait_send()
-    bulk(s_b, r_b, 3, 2).wait_send()
+    bulk(s_b, r_b, 1, 2).wait_send()
+    bulk(s_c, r_c, 2, 6).wait_send()
     tables.wait_send()
     bulk(s_o, r_o, 2, 3).wait_send()
     bulk(s_e, r_e, 1, 4).wait_send()
@@ -714,7 +725,7 @@
                 vmem(2, parts),
                 vmem(*square),
             ]
-            + [vmem(parts * 8, 128)] * 8
+            + [vmem(parts * 8, 128)] * 10
             + [vmem(8, 128), vmem(parts // RUN, RUN * 8, 128)]
             + [vmem(parts * 8, 128)] * 5
             + [
@@ -751,8 +762,8 @@
                 vmem(2, SENT // 4, EDGE, 128),
                 vmem(2, 3, SENT // 4, EDGE, 128),
                 dma((22,)),
-                dma((6,)),
-                dma((6,)),
+                dma((7,)),
+                dma((7,)),
                 dma((2, 2)),
                 dma((2, 2)),
                 dma((6,)),

time: 76.4 us -> 75.3 us (0.986)
  Pallas kernels: 73.2 us -> 71.8 us
    pallas_call x1, Pallas kernels: 73.2 us -> 71.8 us  [shards(): pl.pallas_call(functools.partial(kernel, groups, parts), out_shape=(vmem(...]
where the time goes in v4:
time: 75.3 us; the launch traced here: 74.3 us
  Pallas kernels  71.8 us (95%)
  local copies, waits for them, and re-layouts  1.85 us (2%)
    pallas_call x1, Pallas kernels, shards(): pl.pallas_call(functools.partial(kernel, groups, parts), out_shape=(vmem(...  71.8 us
    unnamed x3, local copies, waits for them, and re-layouts  1.85 us

profile of v4, /device:TPU:56, one launch (start us, length us, event | category | flops | bytes accessed | tf_op | source)
XLA Modules:
  0.0 74.3 jit_solution(1129005731065723870)
XLA Ops:
  0.6 71.8 %shard_map.112 = (f32[3,32,128]{2,1,0:T(8,128)S(1)}, f32[32,128]{1,0:T(8,128)S(1)}, f32[3,32,128]{2,1,0:T(8,128)S(1)}) custom-call(f32[3,32,128]{2,1,0:T(8,128)} %up_h.1, f32[3,32,128]{2,1,0:T(8,128)} %un_h.1, f32[3,3,32,128]{3,2,1,0:T(8,128)} %mem_h.1, f32[32,128]{1,0:T(8,128)} %mod_h.1, f32[3,32,128]{2,1,0:T(8,128)} %q_h.1, f32[8,3,32,128]{3,2,1,0:T(8,128)} %adj_h.1, ...), custom_call_target="tpu_custom_call" | custom-call | tf_op jit(solution)/shard_map/pallas_call | solution.py:716
  72.5 0.6 copy.15
  73.1 0.6 copy.16
  73.7 0.6 copy.17
